TPU v7x, 512 devices: a whole 4x8x8 slice. The times are simulated.
512 devices in a mesh: dp: 64 (over x, z, core), tensor: 8 (over y).
Axes of the slice: x: 4, y: 8, z: 8, core: 2. Of those that a mesh axis runs over, the one named last changes fastest.
Arguments:
- instances: bfloat16 [8192, 1024], P('dp', 'tensor'), may hold values from -6 to 6
- cluster_weights: bfloat16 [128, 256, 1024], P('dp', None, 'tensor'), may hold values from -0.1875 to 0.1875
- cluster_home: int32 [128], replicated, may hold values from 0 to 127, each once
- shortlist: int32 [8192, 20], P('dp'), may hold values from 0 to 127, all different within a row; in each aligned block of 128 rows (0 to 127, 128 to 255, ...) at most 40 rows name the same one
- positives: int32 [8192, 32], P('dp'), may hold values from 0 to 5119
Outputs:
- instance_grad: bfloat16 [8192, 1024], P('dp', 'tensor')
- weight_grad: bfloat16 [128, 256, 1024], P('dp', None, 'tensor')
Inputs may be any that keep to these rules, and one draw needn't show every extreme that they name: `shortlist`: each row names 20 different clusters. Within the rows of one index of dp (aligned blocks of 128 rows) no cluster is named by more than 40 rows, a bound that some block reaches. Every cluster is named somewhere. `cluster_home`: each cluster has its own storage row. `positives`: A code may appear more than once in a row.
All inputs are finite; a program needn't handle non-finite values.
Results may differ from a plain program's by a relative error of at most 0.0051.
Values may be sent and summed in bfloat16 or wider, within the bound.
No kernel may reach another device: no remote copies, remote signals or barrier semaphores. Data moves between devices by JAX's collectives and lax.ppermute only.
A program may use at most 64 MiB of HBM per device.

v0:
```python
import functools
import math

import jax
import jax.numpy as jnp
from jax import lax
from jax.experimental import pallas as pl
from jax.experimental.pallas import tpu as pltpu
from jax.sharding import Mesh, PartitionSpec as P

NX, NZ, NC = 4, 8, 2
LABEL_BITS = 8


def prep_kernel(ids_ref, home_ref, short_ref, pos_ref, out_ref, full_ref):
    short = short_ref[...]
    pos = pos_ref[...]
    picks, rows = short.shape

    def look(c, slots):
        return jnp.where(short == c, home_ref[c], slots)

    slots = lax.fori_loop(0, home_ref.shape[0], look, jnp.zeros_like(short), unroll=8)
    pick = lax.shift_right_logical(pos, LABEL_BITS)
    pos_slot = jnp.zeros_like(pos)
    for k in range(picks):
        pos_slot = jnp.where(pick == k, slots[k : k + 1, :], pos_slot)
    label = pos & ((1 << LABEL_BITS) - 1)
    pad = jnp.full((128 - picks - 2 * pos.shape[0], rows), -1, jnp.int32)
    facts = jnp.concatenate([pos_slot, label, slots, pad], axis=0).astype(jnp.float32)
    full_ref[...] = facts.T.astype(jnp.bfloat16)
    share = out_ref.shape[0]
    out_ref[...] = full_ref[pl.ds(pl.multiple_of(ids_ref[1] * share, share), share), :]


def main_kernel(n_pos, n_picks, first, ids_ref, *refs):
    if first:
        x_ref, w_ref, ig_ref, wg_ref = refs
    else:
        x_ref, w_ref, wg_in_ref, ig_ref, wg_ref = refs
    tiles, feats = x_ref.shape[0], x_ref.shape[1] - 1
    rows = tiles * x_ref.shape[2]
    labels = w_ref.shape[1]
    x = jnp.concatenate([x_ref[:, f].reshape(rows, 128) for f in range(feats)], axis=1)
    w = jnp.concatenate([w_ref[f] for f in range(feats)], axis=1)
    scores = lax.dot_general(w, x, (((1,), (1,)), ((), ())), preferred_element_type=jnp.float32)

    facts = x_ref[:, feats].reshape(rows, 128).astype(jnp.float32).T.astype(jnp.int32)
    base = ids_ref[0] * 2
    pos_slot = facts[:n_pos] - base
    label = facts[n_pos : 2 * n_pos]
    slots = facts[2 * n_pos : 2 * n_pos + 24] - base
    held = (pos_slot == 0) | (pos_slot == 1)
    key = jnp.where(held, pos_slot * (labels // 2) + label, -1)
    word, bit = key >> 5, jnp.left_shift(jnp.int32(1), key & 31)
    lines = lax.broadcasted_iota(jnp.int32, (labels // 32, rows), 0)
    words = jnp.zeros((labels // 32, rows), jnp.int32)
    for p in range(n_pos):
        words = words | jnp.where(word[p : p + 1] == lines, bit[p : p + 1], 0)
    shifts = lax.broadcasted_iota(jnp.int32, (labels // 32, 32, rows), 1)
    bits = lax.shift_right_logical(jnp.broadcast_to(words[:, None, :], shifts.shape), shifts) & 1
    targets = bits.reshape(labels, rows).astype(jnp.float32)
    grad = jax.nn.sigmoid(scores) - targets
    halves = []
    for j in range(2):
        named = jnp.max((slots == j).astype(jnp.float32), axis=0, keepdims=True)
        halves.append(grad[j * (labels // 2) : (j + 1) * (labels // 2)] * named)
    grad = jnp.concatenate(halves, axis=0).astype(jnp.bfloat16)

    ig = lax.dot_general(grad, w, (((0,), (0,)), ((), ())), preferred_element_type=jnp.float32)
    ig = ig.astype(ig_ref.dtype)
    wg = jnp.dot(grad, x, preferred_element_type=jnp.float32)

    @pl.when(pl.program_id(0) == 0)
    def _():
        if first:
            wg_ref[...] = jnp.zeros_like(wg_ref)
        else:
            wg_ref[...] = wg_in_ref[...]

    for f in range(feats):
        ig_ref[:, f] = ig[:, f * 128 : (f + 1) * 128].reshape(tiles, -1, 128)
        wg_ref[f] += wg[:, f * 128 : (f + 1) * 128]


def gradients(ids, x, w, wg, out_type, n_pos, n_picks, steps):
    blocks, width, sub, _ = x.shape
    feats, labels, _ = w.shape
    tiles = blocks // steps
    first = wg is None
    whole = pl.BlockSpec((feats, labels, 128), lambda i, s: (0, 0, 0))
    in_specs = [pl.BlockSpec((tiles, width, sub, 128), lambda i, s: (i, 0, 0, 0)), whole]
    operands = [x, w]
    if not first:
        in_specs.append(whole)
        operands.append(wg)
    flops = 6 * blocks * sub * feats * 128 * labels
    return pl.pallas_call(
        functools.partial(main_kernel, n_pos, n_picks, first),
        out_shape=(
            jax.ShapeDtypeStruct((blocks, feats, sub, 128), out_type),
            jax.ShapeDtypeStruct((feats, labels, 128), jnp.float32),
        ),
        grid_spec=pltpu.PrefetchScalarGridSpec(
            num_scalar_prefetch=1,
            grid=(steps,),
            in_specs=in_specs,
            out_specs=(pl.BlockSpec((tiles, feats, sub, 128), lambda i, s: (i, 0, 0, 0)), whole),
        ),
        compiler_params=pltpu.CompilerParams(vmem_limit_bytes=40 * 1024 * 1024),
        cost_estimate=pl.CostEstimate(flops=flops, bytes_accessed=6 << 20, transcendentals=blocks * sub * labels),
    )(ids, *operands)


def spread(block, axis, size):
    copies = jnp.broadcast_to(block[None], (size, *block.shape))
    return lax.all_to_all(copies, axis, split_axis=0, concat_axis=0, tiled=True)


def collect(parts, axis):
    got = lax.all_to_all(parts.astype(jnp.bfloat16), axis, split_axis=0, concat_axis=0, tiled=True)
    return jnp.sum(got.astype(jnp.float32), axis=0)


def shards(instances, cluster_weights, cluster_home, shortlist, positives):
    ny = lax.axis_size("y")
    rows, part = instances.shape
    owned, labels, _ = cluster_weights.shape
    picks, n_pos = shortlist.shape[1], positives.shape[1]
    clusters = cluster_home.shape[0]
    share = rows // ny
    scale = 1.0 / math.sqrt(rows * picks // owned)
    ids = jnp.stack([lax.axis_index(("x", "z", "c")), lax.axis_index("y")]).astype(jnp.int32)

    w = lax.all_gather(cluster_weights.reshape(owned * labels, part), "y", axis=0)

    facts = pl.pallas_call(
        prep_kernel,
        out_shape=jax.ShapeDtypeStruct((share, 128), jnp.bfloat16),
        in_specs=[pl.BlockSpec(memory_space=pltpu.SMEM)] * 2 + [pl.BlockSpec(memory_space=pltpu.VMEM)] * 2,
        out_specs=pl.BlockSpec(memory_space=pltpu.VMEM),
        scratch_shapes=[pltpu.VMEM((rows, 128), jnp.bfloat16)],
    )(ids, cluster_home, shortlist.T, positives.T)

    own = lax.all_to_all(instances.reshape(ny, share, part), "y", split_axis=0, concat_axis=0, tiled=True)
    own = jnp.concatenate([own, facts[None]], axis=0)
    line = spread(own, "z", NZ)
    mine = spread(line, "x", NX).reshape(NX * NZ, ny + 1, share, 128)
    swap = [(0, 1), (1, 0)]
    theirs = lax.ppermute(mine, "c", swap)

    ig_mine, wg = gradients(ids, mine, w, None, jnp.float32, n_pos, picks, 2)
    ig_theirs, wg = gradients(ids, theirs, w, wg, jnp.bfloat16, n_pos, picks, 2)

    weight_sum = lax.psum_scatter(wg, "y", scatter_dimension=0)
    ig = ig_mine + lax.ppermute(ig_theirs, "c", swap).astype(jnp.float32)
    ig = collect(ig.reshape(NX, NZ, ny, share, 128), "x")
    ig = collect(ig, "z").astype(jnp.bfloat16)
    ig = lax.all_to_all(ig, "y", split_axis=0, concat_axis=0, tiled=True)
    weight_grad = (weight_sum * scale).astype(jnp.bfloat16).reshape(owned, labels, part)
    return ig.reshape(rows, part), weight_grad


def solution(mesh):
    fine = Mesh(mesh.devices.reshape(NX, NZ, NC, -1), ("x", "z", "c", "y"))
    dp = ("x", "z", "c")
    return jax.shard_map(
        shards,
        mesh=fine,
        in_specs=(P(dp, "y"), P(dp, None, "y"), P(), P(dp, None), P(dp, None)),
        out_specs=(P(dp, "y"), P(dp, None, "y")),
        check_vma=False,
    )
```

profile of v0, /device:TPU:6, one launch (start us, length us, event | category | flops | bytes accessed | tf_op | source)
XLA Modules:
  0.0 160.4 jit_solution(6608228721595651943)
XLA Ops:
  7.2 7.1 %all-to-all-start = ((bf16[8,16,128]{2,1,0:T(8,128)(2,1)}), bf16[8,16,128]{2,1,0:T(8,128)(2,1)S(1)}, u32[]{:S(2)}, u32[]{:S(2)}) async-start(bf16[8,16,128]{2,1,0:T(8,128)(2,1)} %bitcast.17), calls=%async_computation | async-start | bytes 65536 | tf_op jit(solution)/shard_map/all_to_all | solution.py:145
  14.3 0.6 pad_add_fusion.ids_ref
  14.9 1.6 %shard_map.68 = bf16[16,128]{1,0:T(8,128)(2,1)} custom-call(s32[2]{0:T(128)} %pad_add_fusion.ids_ref, s32[128]{0:T(128)} %home_ref.1, s32[20,128]{1,0:T(8,128)} %bitcast.20, s32[32,128]{1,0:T(8,128)} %bitcast.19), custom_call_target="tpu_custom_call" | custom-call | tf_op jit(solution)/shard_map/pallas_call | solution.py:137
  16.5 5.8 %all-to-all-done = bf16[8,16,128]{2,1,0:T(8,128)(2,1)S(1)} async-done(((bf16[8,16,128]{2,1,0:T(8,128)(2,1)}), bf16[8,16,128]{2,1,0:T(8,128)(2,1)S(1)}, u32[]{:S(2)}, u32[]{:S(2)}) %all-to-all-start) | async-done | bytes 32800 | tf_op jit(solution)/shard_map/all_to_all | solution.py:145
  22.3 0.7 pad_maximum_fusion
  23.0 21.3 %all_to_all.30 = bf16[8,9,16,128]{3,2,1,0:T(8,128)(2,1)S(1)} all-to-all(bf16[8,9,16,128]{3,2,1,0:T(8,128)(2,1)S(1)} %broadcast_in_dim.7), channel_id=1, replica_groups=mesh['x'=4,'z'=8,'c'=2,'y'=8] {'z'}, dimensions={0} | all-to-all | bytes 589824 | tf_op jit(solution)/shard_map/all_to_all | solution.py:117
  44.3 0.0 copy-start
  44.3 1.2 broadcast_in_dim.8
  45.5 4.8 %all-to-all-start.2 = ((bf16[4,8,9,16,128]{4,3,2,1,0:T(8,128)(2,1)}), bf16[4,8,9,16,128]{4,3,2,1,0:T(8,128)(2,1)S(1)}, u32[]{:S(2)}, u32[]{:S(2)}) async-start(bf16[4,8,9,16,128]{4,3,2,1,0:T(8,128)(2,1)} %broadcast_in_dim.8), calls=%async_computation.2 | async-start | bytes 2359296 | tf_op jit(solution)/shard_map/all_to_all | solution.py:117
  50.3 0.0 all-gather.2.cloned.1.call-start
  50.3 0.7 all-gather.2.cloned.1.call-update
  51.0 0.0 reduce-scatter.2.cloned.1.call-start
  51.0 10.7 %all-to-all-done.2 = bf16[4,8,9,16,128]{4,3,2,1,0:T(8,128)(2,1)S(1)} async-done(((bf16[4,8,9,16,128]{4,3,2,1,0:T(8,128)(2,1)}), bf16[4,8,9,16,128]{4,3,2,1,0:T(8,128)(2,1)S(1)}, u32[]{:S(2)}, u32[]{:S(2)}) %all-to-all-start.2) | async-done | bytes 1179680 | tf_op jit(solution)/shard_map/all_to_all | solution.py:117
  61.7 1.9 %collective-permute-start = (bf16[32,9,16,128]{3,2,1,0:T(8,128)(2,1)S(1)}, bf16[32,9,16,128]{3,2,1,0:T(8,128)(2,1)}, u32[]{:S(2)}, u32[]{:S(2)}) collective-permute-start(bf16[32,9,16,128]{3,2,1,0:T(8,128)(2,1)S(1)} %bitcast.11), channel_id=1, source_target_pairs={{0,8},{8,0},{1,9},{9,1},{2,10},{10,2},{3,11},{11,3},{4,12},{12,4},... | collective-permute-start | bytes 3538952 | tf_op jit(solution)/shard_map/ppermute | solution.py:150
  63.6 21.8 %all-gather.2.cloned.1.call-done.refs_1_ = bf16[8,512,128]{2,1,0:T(8,128)(2,1)} async-done(((bf16[1,512,128]{2,1,0:T(8,128)(2,1)}), bf16[8,512,128]{2,1,0:T(8,128)(2,1)}) %all-gather.2.cloned.1.call-update) | async-done | bytes 1048592 | tf_op jit(solution)/shard_map/all_gather | solution.py:135
  85.4 0.0 copy-done
  85.4 0.0 copy-start.1
  85.4 1.2 copy-done.1
  86.6 4.6 %shard_map.69 = (f32[32,8,16,128]{3,2,1,0:T(8,128)S(1)}, f32[8,512,128]{2,1,0:T(8,128)S(1)}) custom-call(s32[2]{0:T(128)S(1)} %copy-done, bf16[32,9,16,128]{3,2,1,0:T(8,128)(2,1)S(1)} %bitcast.12, bf16[8,512,128]{2,1,0:T(8,128)(2,1)S(1)} %copy-done.1), custom_call_target="tpu_custom_call" | custom-call | flops 1610612736 | bytes 6291456 | tf_op jit(solution)/shard_map/pallas_call | solution.py:98
  91.2 0.0 collective-permute-done.refs_0_
  91.2 6.9 %shard_map.70 = (bf16[32,8,16,128]{3,2,1,0:T(8,128)(2,1)S(1)}, f32[8,512,128]{2,1,0:T(8,128)}) custom-call(s32[2]{0:T(128)S(1)} %copy-done, bf16[32,9,16,128]{3,2,1,0:T(8,128)(2,1)} %collective-permute-done.refs_0_, bf16[8,512,128]{2,1,0:T(8,128)(2,1)S(1)} %copy-done.1, f32[8,512,128]{2,1,0:T(8,128)S(1)} %get-tuple-element.7.refs_2_), custom_call_target="tpu_custom_call" | custom-call | flops 1610612736 | bytes 6291456 | tf_op jit(solution)/shard_map/pallas_call | solution.py:98
  98.2 0.0 reduce-scatter.2.cloned.1.call-update
  98.2 1.9 %collective-permute-start.1 = (bf16[32,8,16,128]{3,2,1,0:T(8,128)(2,1)S(1)}, bf16[32,8,16,128]{3,2,1,0:T(8,128)(2,1)S(1)}, u32[]{:S(2)}, u32[]{:S(2)}) collective-permute-start(bf16[32,8,16,128]{3,2,1,0:T(8,128)(2,1)S(1)} %get-tuple-element.8), channel_id=1, source_target_pairs={{0,8},{8,0},{1,9},{9,1},{2,10},{10,2},{3,11},{11,3},{4,12},{12,4},... | collective-permute-start | bytes 3145736 | tf_op jit(solution)/shard_map/ppermute | solution.py:156
  100.1 2.6 %collective-permute-done.1 = bf16[32,8,16,128]{3,2,1,0:T(8,128)(2,1)S(1)} collective-permute-done((bf16[32,8,16,128]{3,2,1,0:T(8,128)(2,1)S(1)}, bf16[32,8,16,128]{3,2,1,0:T(8,128)(2,1)S(1)}, u32[]{:S(2)}, u32[]{:S(2)}) %collective-permute-start.1) | collective-permute-done | bytes 1048608 | tf_op jit(solution)/shard_map/ppermute | solution.py:156
  102.8 0.4 add_convert_fusion
  103.1 17.9 %all_to_all.31 = bf16[4,8,8,16,128]{4,3,2,1,0:T(8,128)(2,1)S(1)} all-to-all(bf16[4,8,8,16,128]{4,3,2,1,0:T(8,128)(2,1)S(1)} %bitcast.13), channel_id=1, replica_groups=mesh['x'=4,'z'=8,'c'=2,'y'=8] {'x'}, dimensions={0} | all-to-all | bytes 2097152 | tf_op jit(solution)/shard_map/all_to_all | solution.py:121
  121.0 0.2 reduce_sum.24
  121.2 17.9 %all_to_all.32 = bf16[8,8,16,128]{3,2,1,0:T(8,128)(2,1)S(1)} all-to-all(bf16[8,8,16,128]{3,2,1,0:T(8,128)(2,1)S(1)} %reduce_sum.24), channel_id=1, replica_groups=mesh['x'=4,'z'=8,'c'=2,'y'=8] {'z'}, dimensions={0} | all-to-all | bytes 524288 | tf_op jit(solution)/shard_map/all_to_all | solution.py:121
  139.2 12.2 %all_to_all.33 = bf16[8,16,128]{2,1,0:T(8,128)(2,1)S(1)} all-to-all(bf16[8,16,128]{2,1,0:T(8,128)(2,1)S(1)} %reduce_sum.25), channel_id=1, replica_groups=mesh['x'=4,'z'=8,'c'=2,'y'=8] {'y'}, dimensions={0} | all-to-all | bytes 65536 | tf_op jit(solution)/shard_map/all_to_all | solution.py:159
  151.4 0.0 reduce-scatter.2.cloned.1.call-done
  151.4 1.6 %multiply_convert_fusion = bf16[1,512,128]{2,1,0:T(8,128)(2,1)} fusion(f32[1,512,128]{2,1,0:T(8,128)} %reduce-scatter.2.cloned.1.call-done), kind=kLoop, calls=%fused_computation.1 | loop fusion | flops 131072 | bytes 393216 | tf_op jit(solution)/shard_map/convert_element_type | solution.py:160
  153.0 0.6 copy.8
  (2 shorter events, 0.1 us)
Async XLA Ops:
  7.2 15.1 %all-to-all-start = ((bf16[8,16,128]{2,1,0:T(8,128)(2,1)}), bf16[8,16,128]{2,1,0:T(8,128)(2,1)S(1)}, u32[]{:S(2)}, u32[]{:S(2)}) async-start(bf16[8,16,128]{2,1,0:T(8,128)(2,1)} %bitcast.17), calls=%async_computation | async-start | bytes 65536 | tf_op jit(solution)/shard_map/all_to_all | solution.py:145
  44.3 41.1 %copy-start = (s32[2]{0:T(128)S(1)}, s32[2]{0:T(128)}, u32[]{:S(2)}) copy-start(s32[2]{0:T(128)} %pad_add_fusion.ids_ref) | copy-start | bytes 28
  45.5 16.2 %all-to-all-start.2 = ((bf16[4,8,9,16,128]{4,3,2,1,0:T(8,128)(2,1)}), bf16[4,8,9,16,128]{4,3,2,1,0:T(8,128)(2,1)S(1)}, u32[]{:S(2)}, u32[]{:S(2)}) async-start(bf16[4,8,9,16,128]{4,3,2,1,0:T(8,128)(2,1)} %broadcast_in_dim.8), calls=%async_computation.2 | async-start | bytes 2359296 | tf_op jit(solution)/shard_map/all_to_all | solution.py:117
  50.3 35.1 %all-gather.2.cloned.1.call-start = ((), (), s32[]{:S(2)}) async-start(), calls=%async_computation.7 | async-start | bytes 1179648 | tf_op jit(solution)/shard_map/all_gather | solution.py:135
  51.0 100.4 %reduce-scatter.2.cloned.1.call-start = ((), (), s32[]{:S(2)}) async-start(), calls=%async_computation.8 | async-start | bytes 2359296 | tf_op jit(solution)/shard_map/reduce_scatter | solution.py:155
  61.7 29.5 %collective-permute-start = (bf16[32,9,16,128]{3,2,1,0:T(8,128)(2,1)S(1)}, bf16[32,9,16,128]{3,2,1,0:T(8,128)(2,1)}, u32[]{:S(2)}, u32[]{:S(2)}) collective-permute-start(bf16[32,9,16,128]{3,2,1,0:T(8,128)(2,1)S(1)} %bitcast.11), channel_id=1, source_target_pairs={{0,8},{8,0},{1,9},{9,1},{2,10},{10,2},{3,11},{11,3},{4,12},{12,4},... | collective-permute-start | bytes 3538952 | tf_op jit(solution)/shard_map/ppermute | solution.py:150
  85.4 1.2 copy-start.1
  98.2 4.6 %collective-permute-start.1 = (bf16[32,8,16,128]{3,2,1,0:T(8,128)(2,1)S(1)}, bf16[32,8,16,128]{3,2,1,0:T(8,128)(2,1)S(1)}, u32[]{:S(2)}, u32[]{:S(2)}) collective-permute-start(bf16[32,8,16,128]{3,2,1,0:T(8,128)(2,1)S(1)} %get-tuple-element.8), channel_id=1, source_target_pairs={{0,8},{8,0},{1,9},{9,1},{2,10},{10,2},{3,11},{11,3},{4,12},{12,4},... | collective-permute-start | bytes 3145736 | tf_op jit(solution)/shard_map/ppermute | solution.py:156
Sparse Core Ops, SparseCore 0:
  53.2 32.1 all-gather.1
  98.3 43.0 reduce-scatter.1
where the time goes:
time: 162 us; the launch traced here: 160 us
  blocking collectives  69.2 us (43%)
  waiting for transfers between devices  41.6 us (26%)
  starting transfers between devices  15.8 us (10%)
  between operations  14.1 us (9%)
  Pallas kernels  13.2 us (8%)
  other arithmetic  3.5 us (2%)
  local copies, waits for them, and re-layouts  3.07 us (2%)
    all_to_all x2, blocking collectives, collect(): lax.all_to_all(parts.astype(jnp.bfloat16), axis, split_axis=0, concat_axi...  35.8 us
    all_gather x1, waiting for transfers between devices, shards(): lax.all_gather(cluster_weights.reshape(owned * labels, part), 'y', axis=0)  21.8 us
    all_to_all x1, blocking collectives, spread(): return lax.all_to_all(copies, axis, split_axis=0, concat_axis=0, tiled=True)  21.3 us
    all_to_all x1, blocking collectives, shards(): ig = lax.all_to_all(ig, 'y', split_axis=0, concat_axis=0, tiled=True)  12.2 us
    pallas_call x2, Pallas kernels, gradients(): pl.pallas_call(functools.partial(main_kernel, n_pos, n_picks, first), out...  11.5 us
    all_to_all x1, waiting for transfers between devices, spread(): return lax.all_to_all(copies, axis, split_axis=0, concat_axis=0, tiled=True)  10.7 us
    all_to_all x1, starting transfers between devices, shards(): lax.all_to_all(instances.reshape(ny, share, part), 'y', split_axis=0, con...  7.11 us
    all_to_all x1, waiting for transfers between devices, shards(): lax.all_to_all(instances.reshape(ny, share, part), 'y', split_axis=0, con...  5.81 us
  transfers between devices with their start and end apart: 6, of which 4 were waited for; matrix products, arithmetic and copies ran while one was open for 1% of the time, Pallas kernels for 4%

commit v1 on v0

--- a/solution.py
+++ b/solution.py
@@ -12,7 +12,7 @@
 LABEL_BITS = 8
 
 
-def prep_kernel(ids_ref, home_ref, short_ref, pos_ref, out_ref, full_ref):
+def prep_kernel(ids_ref, home_ref, short_ref, pos_ref, x_ref, out_ref):
     short = short_ref[...]
     pos = pos_ref[...]
     picks, rows = short.shape
@@ -27,17 +27,46 @@
         pos_slot = jnp.where(pick == k, slots[k : k + 1, :], pos_slot)
     label = pos & ((1 << LABEL_BITS) - 1)
     pad = jnp.full((128 - picks - 2 * pos.shape[0], rows), -1, jnp.int32)
-    facts = jnp.concatenate([pos_slot, label, slots, pad], axis=0).astype(jnp.float32)
-    full_ref[...] = facts.T.astype(jnp.bfloat16)
-    share = out_ref.shape[0]
-    out_ref[...] = full_ref[pl.ds(pl.multiple_of(ids_ref[1] * share, share), share), :]
+    facts = jnp.concatenate([pos_slot, label, slots, pad], axis=0).astype(jnp.float32).T
+    copies, parts = out_ref.shape[0], out_ref.shape[1]
+    share = rows // parts
+    x = x_ref[...].astype(jnp.float32)
+    line = lax.broadcasted_iota(jnp.int32, (8, 128), 0)
+    for t in range(parts):
+        known = []
+        for i in range(share // 8):
+            tile = facts[t * share + i * 8 : t * share + i * 8 + 8]
+            known.append(jnp.sum(jnp.where(line == ids_ref[1], tile, 0.0), axis=0, keepdims=True))
+        pairs = [x[t * share + j : t * share + j + 2] for j in range(0, share, 2)]
+        message = jnp.concatenate([*pairs, jnp.concatenate(known, axis=0)], axis=1).astype(out_ref.dtype)
+        for c in range(copies):
+            out_ref[c, t] = message
+
+
+def repack_kernel(in_ref, out_ref):
+    copies, zs, _, share, _ = out_ref.shape
+    feats = in_ref.shape[1]
+    for z in range(zs):
+        known = []
+        for f in range(feats):
+            message = in_ref[z, f].astype(jnp.float32)
+            pairs = [message[:, j * 128 : (j + 1) * 128] for j in range(share // 2)]
+            block = jnp.concatenate(pairs, axis=0).astype(out_ref.dtype)
+            known.append(message[:, share // 2 * 128 :])
+            for c in range(copies):
+                out_ref[c, z, f] = block
+        facts = [k[i : i + 1] for i in range(2) for k in known]
+        facts = jnp.concatenate(facts, axis=0).astype(out_ref.dtype)
+        for c in range(copies):
+            out_ref[c, z, feats] = facts
 
 
 def main_kernel(n_pos, n_picks, first, ids_ref, *refs):
     if first:
         x_ref, w_ref, ig_ref, wg_ref = refs
+        acc_ref = wg_ref
     else:
-        x_ref, w_ref, wg_in_ref, ig_ref, wg_ref = refs
+        x_ref, w_ref, wg_in_ref, ig_ref, wg_ref, acc_ref = refs
     tiles, feats = x_ref.shape[0], x_ref.shape[1] - 1
     rows = tiles * x_ref.shape[2]
     labels = w_ref.shape[1]
@@ -71,16 +100,26 @@
     ig = ig.astype(ig_ref.dtype)
     wg = jnp.dot(grad, x, preferred_element_type=jnp.float32)
 
-    @pl.when(pl.program_id(0) == 0)
-    def _():
-        if first:
-            wg_ref[...] = jnp.zeros_like(wg_ref)
-        else:
-            wg_ref[...] = wg_in_ref[...]
-
+    step = pl.program_id(0)
+    parts = [wg[:, f * 128 : (f + 1) * 128] for f in range(feats)]
     for f in range(feats):
         ig_ref[:, f] = ig[:, f * 128 : (f + 1) * 128].reshape(tiles, -1, 128)
-        wg_ref[f] += wg[:, f * 128 : (f + 1) * 128]
+
+    @pl.when(step == 0)
+    def _():
+        for f in range(feats):
+            acc_ref[f] = parts[f] if first else wg_in_ref[f] + parts[f]
+
+    @pl.when(step > 0)
+    def _():
+        for f in range(feats):
+            acc_ref[f] += parts[f]
+
+    if not first:
+
+        @pl.when(step == pl.num_programs(0) - 1)
+        def _():
+            wg_ref[...] = acc_ref[...].astype(wg_ref.dtype)
 
 
 def gradients(ids, x, w, wg, out_type, n_pos, n_picks, steps):
@@ -99,22 +138,18 @@
         functools.partial(main_kernel, n_pos, n_picks, first),
         out_shape=(
             jax.ShapeDtypeStruct((blocks, feats, sub, 128), out_type),
-            jax.ShapeDtypeStruct((feats, labels, 128), jnp.float32),
+            jax.ShapeDtypeStruct((feats, labels, 128), jnp.float32 if first else jnp.bfloat16),
         ),
         grid_spec=pltpu.PrefetchScalarGridSpec(
             num_scalar_prefetch=1,
             grid=(steps,),
             in_specs=in_specs,
             out_specs=(pl.BlockSpec((tiles, feats, sub, 128), lambda i, s: (i, 0, 0, 0)), whole),
+            scratch_shapes=[] if first else [pltpu.VMEM((feats, labels, 128), jnp.float32)],
         ),
-        compiler_params=pltpu.CompilerParams(vmem_limit_bytes=40 * 1024 * 1024),
+        compiler_params=pltpu.CompilerParams(vmem_limit_bytes=24 * 1024 * 1024),
         cost_estimate=pl.CostEstimate(flops=flops, bytes_accessed=6 << 20, transcendentals=blocks * sub * labels),
     )(ids, *operands)
-
-
-def spread(block, axis, size):
-    copies = jnp.broadcast_to(block[None], (size, *block.shape))
-    return lax.all_to_all(copies, axis, split_axis=0, concat_axis=0, tiled=True)
 
 
 def collect(parts, axis):
@@ -129,36 +164,44 @@
     picks, n_pos = shortlist.shape[1], positives.shape[1]
     clusters = cluster_home.shape[0]
     share = rows // ny
+    wide = (share // 2 + 1) * 128
     scale = 1.0 / math.sqrt(rows * picks // owned)
     ids = jnp.stack([lax.axis_index(("x", "z", "c")), lax.axis_index("y")]).astype(jnp.int32)
 
     w = lax.all_gather(cluster_weights.reshape(owned * labels, part), "y", axis=0)
 
-    facts = pl.pallas_call(
+    smem, vmem = pl.BlockSpec(memory_space=pltpu.SMEM), pl.BlockSpec(memory_space=pltpu.VMEM)
+    own = pl.pallas_call(
         prep_kernel,
-        out_shape=jax.ShapeDtypeStruct((share, 128), jnp.bfloat16),
-        in_specs=[pl.BlockSpec(memory_space=pltpu.SMEM)] * 2 + [pl.BlockSpec(memory_space=pltpu.VMEM)] * 2,
-        out_specs=pl.BlockSpec(memory_space=pltpu.VMEM),
-        scratch_shapes=[pltpu.VMEM((rows, 128), jnp.bfloat16)],
-    )(ids, cluster_home, shortlist.T, positives.T)
-
-    own = lax.all_to_all(instances.reshape(ny, share, part), "y", split_axis=0, concat_axis=0, tiled=True)
-    own = jnp.concatenate([own, facts[None]], axis=0)
-    line = spread(own, "z", NZ)
-    mine = spread(line, "x", NX).reshape(NX * NZ, ny + 1, share, 128)
+        out_shape=jax.ShapeDtypeStruct((NZ, ny, 2, wide), jnp.bfloat16),
+        in_specs=[smem, smem, vmem, vmem, vmem],
+        out_specs=vmem,
+        compiler_params=pltpu.CompilerParams(vmem_limit_bytes=52 * 1024 * 1024),
+    )(ids, cluster_home, shortlist.T, positives.T, instances)
+    line = lax.all_to_all(own.reshape(NZ * ny, 2, wide), ("z", "y"), split_axis=0, concat_axis=0, tiled=True)
+    lines = pl.pallas_call(
+        repack_kernel,
+        out_shape=jax.ShapeDtypeStruct((NX, NZ, ny + 1, share, 128), jnp.bfloat16),
+        in_specs=[vmem],
+        out_specs=vmem,
+        compiler_params=pltpu.CompilerParams(vmem_limit_bytes=8 * 1024 * 1024),
+    )(line.reshape(NZ, ny, 2, wide))
+    mine = lax.all_to_all(lines, "x", split_axis=0, concat_axis=0, tiled=True).reshape(NX * NZ, ny + 1, share, 128)
+    mine, w = lax.optimization_barrier((mine, w))
     swap = [(0, 1), (1, 0)]
     theirs = lax.ppermute(mine, "c", swap)
 
     ig_mine, wg = gradients(ids, mine, w, None, jnp.float32, n_pos, picks, 2)
     ig_theirs, wg = gradients(ids, theirs, w, wg, jnp.bfloat16, n_pos, picks, 2)
-
-    weight_sum = lax.psum_scatter(wg, "y", scatter_dimension=0)
-    ig = ig_mine + lax.ppermute(ig_theirs, "c", swap).astype(jnp.float32)
-    ig = collect(ig.reshape(NX, NZ, ny, share, 128), "x")
-    ig = collect(ig, "z").astype(jnp.bfloat16)
-    ig = lax.all_to_all(ig, "y", split_axis=0, concat_axis=0, tiled=True)
+    back = lax.ppermute(ig_theirs, "c", swap)
+
+    weight_sum = lax.psum_scatter(wg, "y", scatter_dimension=0).astype(jnp.float32)
+    ig = ig_mine + back.astype(jnp.float32)
+    ig = collect(ig.reshape(NX, NZ * ny, share, 128), "x")
+    got = lax.all_to_all(ig.astype(jnp.bfloat16), ("z", "y"), split_axis=0, concat_axis=0, tiled=True)
+    ig = jnp.sum(got.reshape(NZ, rows, part).astype(jnp.float32), axis=0).astype(jnp.bfloat16)
     weight_grad = (weight_sum * scale).astype(jnp.bfloat16).reshape(owned, labels, part)
-    return ig.reshape(rows, part), weight_grad
+    return ig, weight_grad
 
 
 def solution(mesh):

time: 162 us -> 132 us (0.81)
  the two profiles are of different devices: /device:TPU:6 before, /device:TPU:8 now
where the time goes in v1:
time: 132 us; the launch traced here: 131 us
  blocking collectives  68.8 us (52%)
  waiting for transfers between devices  16.2 us (12%)
  between operations  14.1 us (11%)
  starting transfers between devices  12.2 us (9%)
  Pallas kernels  10.7 us (8%)
  other arithmetic  4.76 us (4%)
  local copies, waits for them, and re-layouts  4.05 us (3%)
    all_to_all x1, blocking collectives, shards(): lax.all_to_all(own.reshape(NZ * ny, 2, wide), ('z', 'y'), split_axis=0, c...  33.3 us
    all_to_all x1, blocking collectives, collect(): lax.all_to_all(parts.astype(jnp.bfloat16), axis, split_axis=0, concat_axi...  18.3 us
    all_to_all x1, blocking collectives, shards(): lax.all_to_all(lines, 'x', split_axis=0, concat_axis=0, tiled=True)  17.2 us
    pallas_call x2, Pallas kernels, gradients(): pl.pallas_call(functools.partial(main_kernel, n_pos, n_picks, first), out...  9.65 us
    all_to_all x1, waiting for transfers between devices, shards(): lax.all_to_all(ig.astype(jnp.bfloat16), ('z', 'y'), split_axis=0, concat_...  8.16 us
    all_to_all x1, starting transfers between devices, shards(): lax.all_to_all(ig.astype(jnp.bfloat16), ('z', 'y'), split_axis=0, concat_...  7.82 us
    reduce_scatter x1, waiting for transfers between devices, shards(): lax.psum_scatter(wg, 'y', scatter_dimension=0).astype(jnp.float32)  5.01 us
    unnamed x10, local copies, waits for them, and re-layouts  4.05 us
  transfers between devices with their start and end apart: 5, of which 3 were waited for; matrix products, arithmetic and copies ran while one was open for 3% of the time, Pallas kernels for 4%

profile of v1, /device:TPU:8, one launch (start us, length us, event | category | flops | bytes accessed | tf_op | source)
XLA Modules:
  0.0 131.0 jit_solution(4994047228001186444)
XLA Ops:
  7.2 0.0 all-gather.2.cloned.1.call-start
  7.2 0.7 all-gather.2.cloned.1.call-update
  7.9 0.0 reduce-scatter.2.cloned.1.call-start
  8.0 0.1 pad_add_fusion.ids_ref
  8.0 0.0 copy-start
  8.0 0.8 copy-done
  8.8 0.0 copy-start.1
  8.8 0.7 copy-done.1
  9.5 0.0 copy-start.2
  9.5 0.7 copy-done.2
  10.2 0.0 copy-start.3
  10.2 0.7 copy-done.3
  10.9 0.9 shard_map.68
  11.7 33.3 %all_to_all.20 = bf16[64,2,1152]{2,1,0:T(2,128)(2,1)S(1)} all-to-all(bf16[64,2,1152]{2,1,0:T(2,128)(2,1)S(1)} %bitcast.15), channel_id=1, replica_groups=mesh['x'=4,'z'=8,'c'=2,'y'=8] {'z','y'}, dimensions={0} | all-to-all | bytes 589824 | tf_op jit(solution)/shard_map/all_to_all | solution.py:181
  45.0 0.2 shard_map.69
  45.3 17.2 %all_to_all.21 = bf16[4,8,9,16,128]{4,3,2,1,0:T(8,128)(2,1)S(1)} all-to-all(bf16[4,8,9,16,128]{4,3,2,1,0:T(8,128)(2,1)S(1)} %shard_map.69), channel_id=1, replica_groups=mesh['x'=4,'z'=8,'c'=2,'y'=8] {'x'}, dimensions={0} | all-to-all | bytes 2359296 | tf_op jit(solution)/shard_map/all_to_all | solution.py:189
  62.5 0.0 all-gather.2.cloned.1.call-done.refs_1_
  62.5 1.9 %collective-permute-start = (bf16[32,9,16,128]{3,2,1,0:T(8,128)(2,1)S(1)}, bf16[32,9,16,128]{3,2,1,0:T(8,128)(2,1)S(1)}, u32[]{:S(2)}, u32[]{:S(2)}) collective-permute-start(bf16[32,9,16,128]{3,2,1,0:T(8,128)(2,1)S(1)} %bitcast.13), channel_id=1, source_target_pairs={{0,8},{8,0},{1,9},{9,1},{2,10},{10,2},{3,11},{11,3},{4,12},{12,4},... | collective-permute-start | bytes 3538952 | tf_op jit(solution)/shard_map/ppermute | solution.py:192
  64.4 0.0 copy-start.4
  64.4 1.2 copy-done.4
  65.6 4.3 %shard_map.70 = (f32[32,8,16,128]{3,2,1,0:T(8,128)S(1)}, f32[8,512,128]{2,1,0:T(8,128)S(1)}) custom-call(s32[2]{0:T(128)S(1)} %pad_add_fusion.ids_ref, bf16[32,9,16,128]{3,2,1,0:T(8,128)(2,1)S(1)} %bitcast.14, bf16[8,512,128]{2,1,0:T(8,128)(2,1)S(1)} %copy-done.4), custom_call_target="tpu_custom_call" | custom-call | flops 1610612736 | bytes 6291456 | tf_op jit(solution)/shard_map/pallas_call | solution.py:137
  69.9 0.0 collective-permute-done.refs_0_
  69.9 5.4 %shard_map.71 = (bf16[32,8,16,128]{3,2,1,0:T(8,128)(2,1)S(1)}, bf16[8,512,128]{2,1,0:T(8,128)(2,1)}) custom-call(s32[2]{0:T(128)S(1)} %pad_add_fusion.ids_ref, bf16[32,9,16,128]{3,2,1,0:T(8,128)(2,1)S(1)} %collective-permute-done.refs_0_, bf16[8,512,128]{2,1,0:T(8,128)(2,1)S(1)} %copy-done.4, f32[8,512,128]{2,1,0:T(8,128)S(1)} %get-tuple-element.11.refs_2_), custom_call_target="tpu_custom_call" | custom-call | flops 1610612736 | bytes 6291456 | tf_op jit(solution)/shard_map/pallas_call | solution.py:137
  75.3 2.4 %collective-permute-start.1 = (bf16[32,8,16,128]{3,2,1,0:T(8,128)(2,1)S(1)}, bf16[32,8,16,128]{3,2,1,0:T(8,128)(2,1)}, u32[]{:S(2)}, u32[]{:S(2)}) collective-permute-start(bf16[32,8,16,128]{3,2,1,0:T(8,128)(2,1)S(1)} %get-tuple-element.12), channel_id=1, source_target_pairs={{0,8},{8,0},{1,9},{9,1},{2,10},{10,2},{3,11},{11,3},{4,12},{12,4},... | collective-permute-start | bytes 3145736 | tf_op jit(solution)/shard_map/ppermute | solution.py:196
  77.7 0.0 reduce-scatter.2.cloned.1.call-update
  77.7 2.4 %collective-permute-done.1 = bf16[32,8,16,128]{3,2,1,0:T(8,128)(2,1)} collective-permute-done((bf16[32,8,16,128]{3,2,1,0:T(8,128)(2,1)S(1)}, bf16[32,8,16,128]{3,2,1,0:T(8,128)(2,1)}, u32[]{:S(2)}, u32[]{:S(2)}) %collective-permute-start.1) | collective-permute-done | bytes 1048608 | tf_op jit(solution)/shard_map/ppermute | solution.py:196
  80.1 1.5 %add_convert_fusion = bf16[32,8,16,128]{3,2,1,0:T(8,128)(2,1)S(1)} fusion(f32[32,8,16,128]{3,2,1,0:T(8,128)S(1)} %get-tuple-element.10, bf16[32,8,16,128]{3,2,1,0:T(8,128)(2,1)} %collective-permute-done.1), kind=kLoop, calls=%fused_computation | loop fusion | flops 1572864 | bytes 4194304 | tf_op jit(solution)/shard_map/convert_element_type | solution.py:156
  81.6 18.3 %all_to_all.22 = bf16[4,64,16,128]{3,2,1,0:T(8,128)(2,1)S(1)} all-to-all(bf16[4,64,16,128]{3,2,1,0:T(8,128)(2,1)S(1)} %bitcast.19), channel_id=1, replica_groups=mesh['x'=4,'z'=8,'c'=2,'y'=8] {'x'}, dimensions={0} | all-to-all | bytes 2097152 | tf_op jit(solution)/shard_map/all_to_all | solution.py:156
  100.0 0.9 reduce_sum.24
  100.9 7.8 %all-to-all-start.3 = ((bf16[64,16,128]{2,1,0:T(8,128)(2,1)}), bf16[64,16,128]{2,1,0:T(8,128)(2,1)S(1)}, u32[]{:S(2)}, u32[]{:S(2)}) async-start(bf16[64,16,128]{2,1,0:T(8,128)(2,1)} %reduce_sum.24), calls=%async_computation.3 | async-start | bytes 524288 | tf_op jit(solution)/shard_map/all_to_all | solution.py:201
  108.7 5.0 %reduce-scatter.2.cloned.1.call-done = bf16[1,512,128]{2,1,0:T(8,128)(2,1)} async-done(((bf16[8,512,128]{2,1,0:T(8,128)(2,1)}), bf16[1,512,128]{2,1,0:T(8,128)(2,1)}) %reduce-scatter.2.cloned.1.call-update) | async-done | bytes 131088 | tf_op jit(solution)/shard_map/reduce_scatter | solution.py:198
  113.7 1.6 %multiply_convert_fusion = bf16[1,512,128]{2,1,0:T(8,128)(2,1)} fusion(bf16[1,512,128]{2,1,0:T(8,128)(2,1)} %reduce-scatter.2.cloned.1.call-done), kind=kLoop, calls=%fused_computation.2 | loop fusion | flops 196608 | bytes 262144 | tf_op jit(solution)/shard_map/convert_element_type | solution.py:203
  115.3 8.2 %all-to-all-done.3 = bf16[64,16,128]{2,1,0:T(8,128)(2,1)S(1)} async-done(((bf16[64,16,128]{2,1,0:T(8,128)(2,1)}), bf16[64,16,128]{2,1,0:T(8,128)(2,1)S(1)}, u32[]{:S(2)}, u32[]{:S(2)}) %all-to-all-start.3) | async-done | bytes 262176 | tf_op jit(solution)/shard_map/all_to_all | solution.py:201
  123.5 0.7 bitcast_reduce_fusion
Async XLA Ops:
  7.2 55.3 %all-gather.2.cloned.1.call-start = ((), (), s32[]{:S(2)}) async-start(), calls=%async_computation.5 | async-start | bytes 1179648 | tf_op jit(solution)/shard_map/all_gather | solution.py:171
  7.9 105.8 %reduce-scatter.2.cloned.1.call-start = ((), (), s32[]{:S(2)}) async-start(), calls=%async_computation.6 | async-start | bytes 1179648 | tf_op jit(solution)/shard_map/reduce_scatter | solution.py:198
  8.0 0.8 copy-start
  8.8 0.7 copy-start.1
  9.5 0.7 copy-start.2
  10.2 0.7 copy-start.3
  62.5 7.4 %collective-permute-start = (bf16[32,9,16,128]{3,2,1,0:T(8,128)(2,1)S(1)}, bf16[32,9,16,128]{3,2,1,0:T(8,128)(2,1)S(1)}, u32[]{:S(2)}, u32[]{:S(2)}) collective-permute-start(bf16[32,9,16,128]{3,2,1,0:T(8,128)(2,1)S(1)} %bitcast.13), channel_id=1, source_target_pairs={{0,8},{8,0},{1,9},{9,1},{2,10},{10,2},{3,11},{11,3},{4,12},{12,4},... | collective-permute-start | bytes 3538952 | tf_op jit(solution)/shard_map/ppermute | solution.py:192
  64.4 1.2 copy-start.4
  75.3 4.8 %collective-permute-start.1 = (bf16[32,8,16,128]{3,2,1,0:T(8,128)(2,1)S(1)}, bf16[32,8,16,128]{3,2,1,0:T(8,128)(2,1)}, u32[]{:S(2)}, u32[]{:S(2)}) collective-permute-start(bf16[32,8,16,128]{3,2,1,0:T(8,128)(2,1)S(1)} %get-tuple-element.12), channel_id=1, source_target_pairs={{0,8},{8,0},{1,9},{9,1},{2,10},{10,2},{3,11},{11,3},{4,12},{12,4},... | collective-permute-start | bytes 3145736 | tf_op jit(solution)/shard_map/ppermute | solution.py:196
  100.9 22.6 %all-to-all-start.3 = ((bf16[64,16,128]{2,1,0:T(8,128)(2,1)}), bf16[64,16,128]{2,1,0:T(8,128)(2,1)S(1)}, u32[]{:S(2)}, u32[]{:S(2)}) async-start(bf16[64,16,128]{2,1,0:T(8,128)(2,1)} %reduce_sum.24), calls=%async_computation.3 | async-start | bytes 524288 | tf_op jit(solution)/shard_map/all_to_all | solution.py:201
Sparse Core Ops, SparseCore 0:
  10.1 46.8 all-gather.1
  77.8 35.8 reduce-scatter.1

commit v2 on v1

--- a/solution.py
+++ b/solution.py
@@ -61,18 +61,16 @@
             out_ref[c, z, feats] = facts
 
 
-def main_kernel(n_pos, n_picks, first, ids_ref, *refs):
+def main_kernel(n_pos, first, ids_ref, w_hbm, x_ref, *refs):
     if first:
-        x_ref, w_ref, ig_ref, wg_ref = refs
-        acc_ref = wg_ref
+        ig_ref, wg_ref, w_ref, w_sem = refs
     else:
-        x_ref, w_ref, wg_in_ref, ig_ref, wg_ref, acc_ref = refs
+        wg_in_ref, ig_ref, wg_hbm, w_ref, w_sem, wg_ref, wg_sem = refs
+    get = pltpu.make_async_copy(w_hbm, w_ref, w_sem)
+    get.start()
     tiles, feats = x_ref.shape[0], x_ref.shape[1] - 1
     rows = tiles * x_ref.shape[2]
     labels = w_ref.shape[1]
-    x = jnp.concatenate([x_ref[:, f].reshape(rows, 128) for f in range(feats)], axis=1)
-    w = jnp.concatenate([w_ref[f] for f in range(feats)], axis=1)
-    scores = lax.dot_general(w, x, (((1,), (1,)), ((), ())), preferred_element_type=jnp.float32)
 
     facts = x_ref[:, feats].reshape(rows, 128).astype(jnp.float32).T.astype(jnp.int32)
     base = ids_ref[0] * 2
@@ -86,6 +84,11 @@
     words = jnp.zeros((labels // 32, rows), jnp.int32)
     for p in range(n_pos):
         words = words | jnp.where(word[p : p + 1] == lines, bit[p : p + 1], 0)
+    x = jnp.concatenate([x_ref[:, f].reshape(rows, 128) for f in range(feats)], axis=1)
+
+    get.wait()
+    w = jnp.concatenate([w_ref[f] for f in range(feats)], axis=1)
+    scores = lax.dot_general(w, x, (((1,), (1,)), ((), ())), preferred_element_type=jnp.float32)
     shifts = lax.broadcasted_iota(jnp.int32, (labels // 32, 32, rows), 1)
     bits = lax.shift_right_logical(jnp.broadcast_to(words[:, None, :], shifts.shape), shifts) & 1
     targets = bits.reshape(labels, rows).astype(jnp.float32)
@@ -96,60 +99,46 @@
         halves.append(grad[j * (labels // 2) : (j + 1) * (labels // 2)] * named)
     grad = jnp.concatenate(halves, axis=0).astype(jnp.bfloat16)
 
+    puts = []
+    for f in range(0, feats, 2):
+        wg = jnp.dot(grad, x[:, f * 128 : (f + 2) * 128], preferred_element_type=jnp.float32)
+        for i in range(2):
+            part = wg[:, i * 128 : (i + 1) * 128]
+            wg_ref[f + i] = part if first else wg_in_ref[f + i] + part
+        if not first:
+            puts.append(pltpu.make_async_copy(wg_ref.at[pl.ds(f, 2)], wg_hbm.at[pl.ds(f, 2)], wg_sem.at[f // 2]))
+            puts[-1].start()
     ig = lax.dot_general(grad, w, (((0,), (0,)), ((), ())), preferred_element_type=jnp.float32)
     ig = ig.astype(ig_ref.dtype)
-    wg = jnp.dot(grad, x, preferred_element_type=jnp.float32)
-
-    step = pl.program_id(0)
-    parts = [wg[:, f * 128 : (f + 1) * 128] for f in range(feats)]
     for f in range(feats):
         ig_ref[:, f] = ig[:, f * 128 : (f + 1) * 128].reshape(tiles, -1, 128)
-
-    @pl.when(step == 0)
-    def _():
-        for f in range(feats):
-            acc_ref[f] = parts[f] if first else wg_in_ref[f] + parts[f]
-
-    @pl.when(step > 0)
-    def _():
-        for f in range(feats):
-            acc_ref[f] += parts[f]
-
-    if not first:
-
-        @pl.when(step == pl.num_programs(0) - 1)
-        def _():
-            wg_ref[...] = acc_ref[...].astype(wg_ref.dtype)
-
-
-def gradients(ids, x, w, wg, out_type, n_pos, n_picks, steps):
+    for put in puts:
+        put.wait()
+
+
+def gradients(ids, x, w, wg, out_type, n_pos):
     blocks, width, sub, _ = x.shape
     feats, labels, _ = w.shape
-    tiles = blocks // steps
     first = wg is None
-    whole = pl.BlockSpec((feats, labels, 128), lambda i, s: (0, 0, 0))
-    in_specs = [pl.BlockSpec((tiles, width, sub, 128), lambda i, s: (i, 0, 0, 0)), whole]
-    operands = [x, w]
+    smem, vmem = pl.BlockSpec(memory_space=pltpu.SMEM), pl.BlockSpec(memory_space=pltpu.VMEM)
+    hbm = pl.BlockSpec(memory_space=pltpu.HBM)
+    scratch = [pltpu.VMEM((feats, labels, 128), jnp.bfloat16), pltpu.SemaphoreType.DMA]
     if not first:
-        in_specs.append(whole)
-        operands.append(wg)
-    flops = 6 * blocks * sub * feats * 128 * labels
+        scratch += [pltpu.VMEM((feats, labels, 128), jnp.float32), pltpu.SemaphoreType.DMA((feats // 2,))]
     return pl.pallas_call(
-        functools.partial(main_kernel, n_pos, n_picks, first),
+        functools.partial(main_kernel, n_pos, first),
         out_shape=(
             jax.ShapeDtypeStruct((blocks, feats, sub, 128), out_type),
-            jax.ShapeDtypeStruct((feats, labels, 128), jnp.float32 if first else jnp.bfloat16),
+            jax.ShapeDtypeStruct((feats, labels, 128), jnp.float32),
         ),
-        grid_spec=pltpu.PrefetchScalarGridSpec(
-            num_scalar_prefetch=1,
-            grid=(steps,),
-            in_specs=in_specs,
-            out_specs=(pl.BlockSpec((tiles, feats, sub, 128), lambda i, s: (i, 0, 0, 0)), whole),
-            scratch_shapes=[] if first else [pltpu.VMEM((feats, labels, 128), jnp.float32)],
+        in_specs=[smem, hbm, vmem] + [vmem] * (not first),
+        out_specs=(vmem, vmem if first else hbm),
+        scratch_shapes=scratch,
+        compiler_params=pltpu.CompilerParams(vmem_limit_bytes=28 * 1024 * 1024),
+        cost_estimate=pl.CostEstimate(
+            flops=6 * blocks * sub * feats * 128 * labels, bytes_accessed=6 << 20, transcendentals=blocks * sub * labels
         ),
-        compiler_params=pltpu.CompilerParams(vmem_limit_bytes=24 * 1024 * 1024),
-        cost_estimate=pl.CostEstimate(flops=flops, bytes_accessed=6 << 20, transcendentals=blocks * sub * labels),
-    )(ids, *operands)
+    )(ids, w, x, *([] if first else [wg]))
 
 
 def collect(parts, axis):
@@ -162,7 +151,6 @@
     rows, part = instances.shape
     owned, labels, _ = cluster_weights.shape
     picks, n_pos = shortlist.shape[1], positives.shape[1]
-    clusters = cluster_home.shape[0]
     share = rows // ny
     wide = (share // 2 + 1) * 128
     scale = 1.0 / math.sqrt(rows * picks // owned)
@@ -176,7 +164,6 @@
         out_shape=jax.ShapeDtypeStruct((NZ, ny, 2, wide), jnp.bfloat16),
         in_specs=[smem, smem, vmem, vmem, vmem],
         out_specs=vmem,
-        compiler_params=pltpu.CompilerParams(vmem_limit_bytes=52 * 1024 * 1024),
     )(ids, cluster_home, shortlist.T, positives.T, instances)
     line = lax.all_to_all(own.reshape(NZ * ny, 2, wide), ("z", "y"), split_axis=0, concat_axis=0, tiled=True)
     lines = pl.pallas_call(
@@ -191,11 +178,11 @@
     swap = [(0, 1), (1, 0)]
     theirs = lax.ppermute(mine, "c", swap)
 
-    ig_mine, wg = gradients(ids, mine, w, None, jnp.float32, n_pos, picks, 2)
-    ig_theirs, wg = gradients(ids, theirs, w, wg, jnp.bfloat16, n_pos, picks, 2)
+    ig_mine, wg = gradients(ids, mine, w, None, jnp.float32, n_pos)
+    ig_theirs, wg = gradients(ids, theirs, w, wg, jnp.bfloat16, n_pos)
     back = lax.ppermute(ig_theirs, "c", swap)
 
-    weight_sum = lax.psum_scatter(wg, "y", scatter_dimension=0).astype(jnp.float32)
+    weight_sum = lax.psum_scatter(wg, "y", scatter_dimension=0)
     ig = ig_mine + back.astype(jnp.float32)
     ig = collect(ig.reshape(NX, NZ * ny, share, 128), "x")
     got = lax.all_to_all(ig.astype(jnp.bfloat16), ("z", "y"), split_axis=0, concat_axis=0, tiled=True)

time: 132 us -> 128 us (0.970)
  the two profiles are of different devices: /device:TPU:8 before, /device:TPU:6 now
where the time goes in v2:
time: 128 us; the launch traced here: 127 us
  blocking collectives  92.7 us (72%)
  between operations  14.1 us (11%)
  Pallas kernels  8.36 us (7%)
  starting transfers between devices  4.38 us (3%)
  other arithmetic  3.57 us (3%)
  waiting for transfers between devices  2.97 us (2%)
    all_to_all x1, blocking collectives, shards(): lax.all_to_all(own.reshape(NZ * ny, 2, wide), ('z', 'y'), split_axis=0, c...  34.1 us
    all_to_all x1, blocking collectives, shards(): lax.all_to_all(ig.astype(jnp.bfloat16), ('z', 'y'), split_axis=0, concat_...  25.7 us
    all_to_all x1, blocking collectives, collect(): lax.all_to_all(parts.astype(jnp.bfloat16), axis, split_axis=0, concat_axi...  18.3 us
    all_to_all x1, blocking collectives, shards(): lax.all_to_all(lines, 'x', split_axis=0, concat_axis=0, tiled=True)  14.5 us
    pallas_call x2, Pallas kernels, gradients(): pl.pallas_call(functools.partial(main_kernel, n_pos, first), out_shape=(j...  6.29 us
  transfers between devices with their start and end apart: 4, of which 1 were waited for; matrix products, arithmetic and copies ran while one was open for 2% of the time, Pallas kernels for 4%

profile of v2, /device:TPU:6, one launch (start us, length us, event | category | flops | bytes accessed | tf_op | source)
XLA Modules:
  0.0 127.3 jit_solution(17195407626692816204)
XLA Ops:
  7.2 0.0 all-gather.2.cloned.1.call-start
  7.2 0.7 all-gather.2.cloned.1.call-update
  7.9 0.0 reduce-scatter.2.cloned.1.call-start
  8.0 0.6 pad_add_fusion.ids_ref
  8.6 1.8 %shard_map.68 = bf16[8,8,2,1152]{3,2,1,0:T(2,128)(2,1)} custom-call(s32[2]{0:T(128)} %pad_add_fusion.ids_ref, s32[128]{0:T(128)} %home_ref.1, s32[20,128]{1,0:T(8,128)} %bitcast.22, s32[32,128]{1,0:T(8,128)} %bitcast.21, bf16[128,128]{1,0:T(8,128)(2,1)} %x_ref.1), custom_call_target="tpu_custom_call" | custom-call | tf_op jit(solution)/shard_map/pallas_call | solution.py:162
  10.4 0.0 copy-start
  10.4 34.1 %all_to_all.20 = bf16[64,2,1152]{2,1,0:T(2,128)(2,1)S(1)} all-to-all(bf16[64,2,1152]{2,1,0:T(2,128)(2,1)} %bitcast.17), channel_id=1, replica_groups=mesh['x'=4,'z'=8,'c'=2,'y'=8] {'z','y'}, dimensions={0} | all-to-all | bytes 589824 | tf_op jit(solution)/shard_map/all_to_all | solution.py:168
  44.5 0.2 shard_map.69
  44.8 14.5 %all_to_all.21 = bf16[4,8,9,16,128]{4,3,2,1,0:T(8,128)(2,1)S(1)} all-to-all(bf16[4,8,9,16,128]{4,3,2,1,0:T(8,128)(2,1)S(1)} %shard_map.69), channel_id=1, replica_groups=mesh['x'=4,'z'=8,'c'=2,'y'=8] {'x'}, dimensions={0} | all-to-all | bytes 2359296 | tf_op jit(solution)/shard_map/all_to_all | solution.py:176
  59.3 0.0 all-gather.2.cloned.1.call-done.w_hbm
  59.3 1.9 %collective-permute-start = (bf16[32,9,16,128]{3,2,1,0:T(8,128)(2,1)S(1)}, bf16[32,9,16,128]{3,2,1,0:T(8,128)(2,1)S(1)}, u32[]{:S(2)}, u32[]{:S(2)}) collective-permute-start(bf16[32,9,16,128]{3,2,1,0:T(8,128)(2,1)S(1)} %bitcast.13), channel_id=1, source_target_pairs={{0,8},{8,0},{1,9},{9,1},{2,10},{10,2},{3,11},{11,3},{4,12},{12,4},... | collective-permute-start | bytes 3538952 | tf_op jit(solution)/shard_map/ppermute | solution.py:179
  61.2 0.0 copy-done
  61.2 0.0 copy-start.1
  61.2 1.2 copy-done.1
  62.5 0.0 copy-start.2
  62.5 2.8 %shard_map.70 = (f32[32,8,16,128]{3,2,1,0:T(8,128)S(1)}, f32[8,512,128]{2,1,0:T(8,128)S(1)}) custom-call(s32[2]{0:T(128)S(1)} %copy-done, bf16[8,512,128]{2,1,0:T(8,128)(2,1)S(1)} %copy-done.1, bf16[32,9,16,128]{3,2,1,0:T(8,128)(2,1)S(1)} %bitcast.14), custom_call_target="tpu_custom_call" | custom-call | flops 1610612736 | bytes 6291456 | tf_op jit(solution)/shard_map/pallas_call | solution.py:128
  65.3 0.0 collective-permute-done.x_ref
  65.3 0.0 copy-done.2
  65.3 3.4 %shard_map.71 = (bf16[32,8,16,128]{3,2,1,0:T(8,128)(2,1)S(1)}, f32[8,512,128]{2,1,0:T(8,128)}) custom-call(s32[2]{0:T(128)S(1)} %copy-done, bf16[8,512,128]{2,1,0:T(8,128)(2,1)S(1)} %copy-done.2, bf16[32,9,16,128]{3,2,1,0:T(8,128)(2,1)S(1)} %collective-permute-done.x_ref, f32[8,512,128]{2,1,0:T(8,128)S(1)} %get-tuple-element.11.refs_0_), custom_call_target="tpu_custom_call" | custom-call | flops 1610612736 | bytes 6291456 | tf_op jit(solution)/shard_map/pallas_call | solution.py:128
  68.8 0.0 reduce-scatter.2.cloned.1.call-update
  68.8 2.4 %collective-permute-start.1 = (bf16[32,8,16,128]{3,2,1,0:T(8,128)(2,1)S(1)}, bf16[32,8,16,128]{3,2,1,0:T(8,128)(2,1)S(1)}, u32[]{:S(2)}, u32[]{:S(2)}) collective-permute-start(bf16[32,8,16,128]{3,2,1,0:T(8,128)(2,1)S(1)} %get-tuple-element.12), channel_id=1, source_target_pairs={{0,8},{8,0},{1,9},{9,1},{2,10},{10,2},{3,11},{11,3},{4,12},{12,4},... | collective-permute-start | bytes 3145736 | tf_op jit(solution)/shard_map/ppermute | solution.py:183
  71.2 2.3 %collective-permute-done.1 = bf16[32,8,16,128]{3,2,1,0:T(8,128)(2,1)S(1)} collective-permute-done((bf16[32,8,16,128]{3,2,1,0:T(8,128)(2,1)S(1)}, bf16[32,8,16,128]{3,2,1,0:T(8,128)(2,1)S(1)}, u32[]{:S(2)}, u32[]{:S(2)}) %collective-permute-start.1) | collective-permute-done | bytes 1048608 | tf_op jit(solution)/shard_map/ppermute | solution.py:183
  73.5 0.4 add_convert_fusion
  73.9 18.3 %all_to_all.22 = bf16[4,64,16,128]{3,2,1,0:T(8,128)(2,1)S(1)} all-to-all(bf16[4,64,16,128]{3,2,1,0:T(8,128)(2,1)S(1)} %bitcast.16), channel_id=1, replica_groups=mesh['x'=4,'z'=8,'c'=2,'y'=8] {'x'}, dimensions={0} | all-to-all | bytes 2097152 | tf_op jit(solution)/shard_map/all_to_all | solution.py:145
  92.2 0.3 reduce_sum.24
  92.5 25.7 %all_to_all.23 = bf16[64,16,128]{2,1,0:T(8,128)(2,1)S(1)} all-to-all(bf16[64,16,128]{2,1,0:T(8,128)(2,1)S(1)} %reduce_sum.24), channel_id=1, replica_groups=mesh['x'=4,'z'=8,'c'=2,'y'=8] {'z','y'}, dimensions={0} | all-to-all | bytes 524288 | tf_op jit(solution)/shard_map/all_to_all | solution.py:188
  118.2 0.7 bitcast_reduce_fusion
  118.9 0.0 reduce-scatter.2.cloned.1.call-done
  118.9 1.6 %multiply_convert_fusion = bf16[1,512,128]{2,1,0:T(8,128)(2,1)} fusion(f32[1,512,128]{2,1,0:T(8,128)} %reduce-scatter.2.cloned.1.call-done), kind=kLoop, calls=%fused_computation.2 | loop fusion | flops 131072 | bytes 393216 | tf_op jit(solution)/shard_map/convert_element_type | solution.py:190
Async XLA Ops:
  7.2 52.1 %all-gather.2.cloned.1.call-start = ((), (), s32[]{:S(2)}) async-start(), calls=%async_computation.5 | async-start | bytes 1179648 | tf_op jit(solution)/shard_map/all_gather | solution.py:159
  7.9 111.0 %reduce-scatter.2.cloned.1.call-start = ((), (), s32[]{:S(2)}) async-start(), calls=%async_computation.6 | async-start | bytes 2359296 | tf_op jit(solution)/shard_map/reduce_scatter | solution.py:185
  10.4 50.8 %copy-start = (s32[2]{0:T(128)S(1)}, s32[2]{0:T(128)}, u32[]{:S(2)}) copy-start(s32[2]{0:T(128)} %pad_add_fusion.ids_ref) | copy-start | bytes 28
  59.3 6.0 %collective-permute-start = (bf16[32,9,16,128]{3,2,1,0:T(8,128)(2,1)S(1)}, bf16[32,9,16,128]{3,2,1,0:T(8,128)(2,1)S(1)}, u32[]{:S(2)}, u32[]{:S(2)}) collective-permute-start(bf16[32,9,16,128]{3,2,1,0:T(8,128)(2,1)S(1)} %bitcast.13), channel_id=1, source_target_pairs={{0,8},{8,0},{1,9},{9,1},{2,10},{10,2},{3,11},{11,3},{4,12},{12,4},... | collective-permute-start | bytes 3538952 | tf_op jit(solution)/shard_map/ppermute | solution.py:179
  61.2 1.2 copy-start.1
  62.5 2.9 %copy-start.2 = (bf16[8,512,128]{2,1,0:T(8,128)(2,1)S(1)}, bf16[8,512,128]{2,1,0:T(8,128)(2,1)}, u32[]{:S(2)}) copy-start(bf16[8,512,128]{2,1,0:T(8,128)(2,1)} %all-gather.2.cloned.1.call-done.w_hbm) | copy-start | bytes 3145732
  68.8 4.7 %collective-permute-start.1 = (bf16[32,8,16,128]{3,2,1,0:T(8,128)(2,1)S(1)}, bf16[32,8,16,128]{3,2,1,0:T(8,128)(2,1)S(1)}, u32[]{:S(2)}, u32[]{:S(2)}) collective-permute-start(bf16[32,8,16,128]{3,2,1,0:T(8,128)(2,1)S(1)} %get-tuple-element.12), channel_id=1, source_target_pairs={{0,8},{8,0},{1,9},{9,1},{2,10},{10,2},{3,11},{11,3},{4,12},{12,4},... | collective-permute-start | bytes 3145736 | tf_op jit(solution)/shard_map/ppermute | solution.py:183
Sparse Core Ops, SparseCore 0:
  10.1 47.2 all-gather.1
  68.9 45.2 reduce-scatter.1

commit v3 on v2

--- a/solution.py
+++ b/solution.py
@@ -12,7 +12,7 @@
 LABEL_BITS = 8
 
 
-def prep_kernel(ids_ref, home_ref, short_ref, pos_ref, x_ref, out_ref):
+def prep_kernel(place_ref, home_ref, short_ref, pos_ref, out_ref, full_ref):
     short = short_ref[...]
     pos = pos_ref[...]
     picks, rows = short.shape
@@ -28,40 +28,34 @@
     label = pos & ((1 << LABEL_BITS) - 1)
     pad = jnp.full((128 - picks - 2 * pos.shape[0], rows), -1, jnp.int32)
     facts = jnp.concatenate([pos_slot, label, slots, pad], axis=0).astype(jnp.float32).T
-    copies, parts = out_ref.shape[0], out_ref.shape[1]
-    share = rows // parts
-    x = x_ref[...].astype(jnp.float32)
-    line = lax.broadcasted_iota(jnp.int32, (8, 128), 0)
-    for t in range(parts):
-        known = []
-        for i in range(share // 8):
-            tile = facts[t * share + i * 8 : t * share + i * 8 + 8]
-            known.append(jnp.sum(jnp.where(line == ids_ref[1], tile, 0.0), axis=0, keepdims=True))
-        pairs = [x[t * share + j : t * share + j + 2] for j in range(0, share, 2)]
-        message = jnp.concatenate([*pairs, jnp.concatenate(known, axis=0)], axis=1).astype(out_ref.dtype)
-        for c in range(copies):
-            out_ref[c, t] = message
+    full_ref[...] = facts
+    share = out_ref.shape[0]
+    first = pl.multiple_of(place_ref[0] * share, share)
+    out_ref[...] = full_ref[pl.ds(first, share), :].astype(out_ref.dtype)
 
 
-def repack_kernel(in_ref, out_ref):
-    copies, zs, _, share, _ = out_ref.shape
-    feats = in_ref.shape[1]
-    for z in range(zs):
-        known = []
-        for f in range(feats):
-            message = in_ref[z, f].astype(jnp.float32)
-            pairs = [message[:, j * 128 : (j + 1) * 128] for j in range(share // 2)]
-            block = jnp.concatenate(pairs, axis=0).astype(out_ref.dtype)
-            known.append(message[:, share // 2 * 128 :])
-            for c in range(copies):
-                out_ref[c, z, f] = block
-        facts = [k[i : i + 1] for i in range(2) for k in known]
-        facts = jnp.concatenate(facts, axis=0).astype(out_ref.dtype)
-        for c in range(copies):
-            out_ref[c, z, feats] = facts
+def copy_kernel(*refs):
+    *in_refs, out_ref = refs
+    for c in range(out_ref.shape[0]):
+        at = 0
+        for ref in in_refs:
+            out_ref[c, at : at + ref.shape[0]] = ref[...]
+            at += ref.shape[0]
 
 
-def main_kernel(n_pos, first, ids_ref, w_hbm, x_ref, *refs):
+def copies(number, *blocks):
+    rest = blocks[0].shape[1:]
+    vmem = pl.BlockSpec(memory_space=pltpu.VMEM)
+    return pl.pallas_call(
+        copy_kernel,
+        out_shape=jax.ShapeDtypeStruct((number, sum(b.shape[0] for b in blocks), *rest), blocks[0].dtype),
+        in_specs=[vmem] * len(blocks),
+        out_specs=vmem,
+        compiler_params=pltpu.CompilerParams(vmem_limit_bytes=8 * 1024 * 1024),
+    )(*blocks)
+
+
+def main_kernel(n_pos, first, me_ref, w_hbm, x_ref, *refs):
     if first:
         ig_ref, wg_ref, w_ref, w_sem = refs
     else:
@@ -73,7 +67,7 @@
     labels = w_ref.shape[1]
 
     facts = x_ref[:, feats].reshape(rows, 128).astype(jnp.float32).T.astype(jnp.int32)
-    base = ids_ref[0] * 2
+    base = me_ref[0] * 2
     pos_slot = facts[:n_pos] - base
     label = facts[n_pos : 2 * n_pos]
     slots = facts[2 * n_pos : 2 * n_pos + 24] - base
@@ -116,7 +110,7 @@
         put.wait()
 
 
-def gradients(ids, x, w, wg, out_type, n_pos):
+def gradients(me, x, w, wg, out_type, n_pos):
     blocks, width, sub, _ = x.shape
     feats, labels, _ = w.shape
     first = wg is None
@@ -138,7 +132,7 @@
         cost_estimate=pl.CostEstimate(
             flops=6 * blocks * sub * feats * 128 * labels, bytes_accessed=6 << 20, transcendentals=blocks * sub * labels
         ),
-    )(ids, w, x, *([] if first else [wg]))
+    )(me, w, x, *([] if first else [wg]))
 
 
 def collect(parts, axis):
@@ -152,34 +146,29 @@
     owned, labels, _ = cluster_weights.shape
     picks, n_pos = shortlist.shape[1], positives.shape[1]
     share = rows // ny
-    wide = (share // 2 + 1) * 128
     scale = 1.0 / math.sqrt(rows * picks // owned)
-    ids = jnp.stack([lax.axis_index(("x", "z", "c")), lax.axis_index("y")]).astype(jnp.int32)
+    me, place = lax.axis_index(("x", "z", "c")).reshape(1), lax.axis_index("y").reshape(1)
 
     w = lax.all_gather(cluster_weights.reshape(owned * labels, part), "y", axis=0)
 
     smem, vmem = pl.BlockSpec(memory_space=pltpu.SMEM), pl.BlockSpec(memory_space=pltpu.VMEM)
-    own = pl.pallas_call(
+    own = lax.all_to_all(instances.reshape(ny, share, part), "y", split_axis=0, concat_axis=0, tiled=True)
+    facts = pl.pallas_call(
         prep_kernel,
-        out_shape=jax.ShapeDtypeStruct((NZ, ny, 2, wide), jnp.bfloat16),
-        in_specs=[smem, smem, vmem, vmem, vmem],
+        out_shape=jax.ShapeDtypeStruct((share, 128), jnp.bfloat16),
+        in_specs=[smem, smem, vmem, vmem],
         out_specs=vmem,
-    )(ids, cluster_home, shortlist.T, positives.T, instances)
-    line = lax.all_to_all(own.reshape(NZ * ny, 2, wide), ("z", "y"), split_axis=0, concat_axis=0, tiled=True)
-    lines = pl.pallas_call(
-        repack_kernel,
-        out_shape=jax.ShapeDtypeStruct((NX, NZ, ny + 1, share, 128), jnp.bfloat16),
-        in_specs=[vmem],
-        out_specs=vmem,
-        compiler_params=pltpu.CompilerParams(vmem_limit_bytes=8 * 1024 * 1024),
-    )(line.reshape(NZ, ny, 2, wide))
+        scratch_shapes=[pltpu.VMEM((rows, 128), jnp.float32)],
+    )(place, cluster_home, shortlist.T, positives.T)
+    line = lax.all_to_all(copies(NZ, own, facts[None]), "z", split_axis=0, concat_axis=0, tiled=True)
+    lines = copies(NX, line)
     mine = lax.all_to_all(lines, "x", split_axis=0, concat_axis=0, tiled=True).reshape(NX * NZ, ny + 1, share, 128)
     mine, w = lax.optimization_barrier((mine, w))
     swap = [(0, 1), (1, 0)]
     theirs = lax.ppermute(mine, "c", swap)
 
-    ig_mine, wg = gradients(ids, mine, w, None, jnp.float32, n_pos)
-    ig_theirs, wg = gradients(ids, theirs, w, wg, jnp.bfloat16, n_pos)
+    ig_mine, wg = gradients(me, mine, w, None, jnp.float32, n_pos)
+    ig_theirs, wg = gradients(me, theirs, w, wg, jnp.bfloat16, n_pos)
     back = lax.ppermute(ig_theirs, "c", swap)
 
     weight_sum = lax.psum_scatter(wg, "y", scatter_dimension=0)

time: 128 us -> 127 us (level)
  blocking collectives: 92.7 us -> 78 us
  starting transfers between devices: 4.38 us -> 11.5 us
  waiting for transfers between devices: 2.97 us -> 9.3 us
    all_to_all x1, blocking collectives: 34.1 us -> 21.3 us  [shards(): lax.all_to_all(copies(NZ, own, facts[None]), 'z', split_axis=0, concat_ax...]
    all_to_all x0 -> x1, starting transfers between devices: none -> 7.11 us  [shards(): lax.all_to_all(instances.reshape(ny, share, part), 'y', split_axis=0, con...]
    all_to_all x0 -> x1, waiting for transfers between devices: none -> 6.34 us  [shards(): lax.all_to_all(instances.reshape(ny, share, part), 'y', split_axis=0, con...]
    all_to_all x1, blocking collectives: 25.7 us -> 22.5 us  [shards(): lax.all_to_all(ig.astype(jnp.bfloat16), ('z', 'y'), split_axis=0, concat_...]
    all_to_all x1, blocking collectives: 14.5 us -> 16 us  [shards(): lax.all_to_all(lines, 'x', split_axis=0, concat_axis=0, tiled=True)]
  transfers between devices with their start and end apart: 4 -> 5, of which waited for: 1 -> 2; matrix products, arithmetic and copies ran while one was open for 2% -> 1% of each run, Pallas kernels for 4% -> 3%
where the time goes in v3:
time: 127 us; the launch traced here: 126 us
  blocking collectives  78 us (61%)
  between operations  14.1 us (11%)
  starting transfers between devices  11.5 us (9%)
  waiting for transfers between devices  9.3 us (7%)
  Pallas kernels  8.32 us (7%)
  other arithmetic  2.92 us (2%)
  local copies, waits for them, and re-layouts  1.9 us (1%)
    all_to_all x1, blocking collectives, shards(): lax.all_to_all(ig.astype(jnp.bfloat16), ('z', 'y'), split_axis=0, concat_...  22.5 us
    all_to_all x1, blocking collectives, shards(): lax.all_to_all(copies(NZ, own, facts[None]), 'z', split_axis=0, concat_ax...  21.3 us
    all_to_all x1, blocking collectives, collect(): lax.all_to_all(parts.astype(jnp.bfloat16), axis, split_axis=0, concat_axi...  18.3 us
    all_to_all x1, blocking collectives, shards(): lax.all_to_all(lines, 'x', split_axis=0, concat_axis=0, tiled=True)  16 us
    all_to_all x1, starting transfers between devices, shards(): lax.all_to_all(instances.reshape(ny, share, part), 'y', split_axis=0, con...  7.11 us
    pallas_call x2, Pallas kernels, gradients(): pl.pallas_call(functools.partial(main_kernel, n_pos, first), out_shape=(j...  6.49 us
    all_to_all x1, waiting for transfers between devices, shards(): lax.all_to_all(instances.reshape(ny, share, part), 'y', split_axis=0, con...  6.34 us
  transfers between devices with their start and end apart: 5, of which 2 were waited for; matrix products, arithmetic and copies ran while one was open for 1% of the time, Pallas kernels for 3%

profile of v3, /device:TPU:6, one launch (start us, length us, event | category | flops | bytes accessed | tf_op | source)
XLA Modules:
  0.0 126.1 jit_solution(13334721615198176956)
XLA Ops:
  7.2 0.0 all-gather.2.cloned.1.call-start
  7.2 0.7 all-gather.2.cloned.1.call-update
  7.9 7.1 %all-to-all-start = ((bf16[8,16,128]{2,1,0:T(8,128)(2,1)}), bf16[8,16,128]{2,1,0:T(8,128)(2,1)S(1)}, u32[]{:S(2)}, u32[]{:S(2)}) async-start(bf16[8,16,128]{2,1,0:T(8,128)(2,1)} %bitcast.20), calls=%async_computation | async-start | bytes 65536 | tf_op jit(solution)/shard_map/all_to_all | solution.py:155
  15.0 0.0 reduce-scatter.2.cloned.1.call-start
  15.1 1.6 %shard_map.68 = bf16[16,128]{1,0:T(8,128)(2,1)} custom-call(s32[1]{0:T(128)} %bitcast.2.place_ref, s32[128]{0:T(128)} %home_ref.1, s32[20,128]{1,0:T(8,128)} %bitcast.22, s32[32,128]{1,0:T(8,128)} %bitcast.21), custom_call_target="tpu_custom_call" | custom-call | tf_op jit(solution)/shard_map/pallas_call | solution.py:156
  16.7 6.3 %all-to-all-done.refs_0_ = bf16[8,16,128]{2,1,0:T(8,128)(2,1)S(1)} async-done(((bf16[8,16,128]{2,1,0:T(8,128)(2,1)}), bf16[8,16,128]{2,1,0:T(8,128)(2,1)S(1)}, u32[]{:S(2)}, u32[]{:S(2)}) %all-to-all-start) | async-done | bytes 32800 | tf_op jit(solution)/shard_map/all_to_all | solution.py:155
  23.0 0.0 copy-start
  23.0 0.7 copy-done
  23.8 21.3 %all_to_all.25.refs_0_ = bf16[8,9,16,128]{3,2,1,0:T(8,128)(2,1)S(1)} all-to-all(bf16[8,9,16,128]{3,2,1,0:T(8,128)(2,1)S(1)} %shard_map.69), channel_id=1, replica_groups=mesh['x'=4,'z'=8,'c'=2,'y'=8] {'z'}, dimensions={0} | all-to-all | bytes 589824 | tf_op jit(solution)/shard_map/all_to_all | solution.py:163
  45.0 0.2 shard_map.70
  45.2 16.0 %all_to_all.26 = bf16[4,8,9,16,128]{4,3,2,1,0:T(8,128)(2,1)S(1)} all-to-all(bf16[4,8,9,16,128]{4,3,2,1,0:T(8,128)(2,1)S(1)} %shard_map.70), channel_id=1, replica_groups=mesh['x'=4,'z'=8,'c'=2,'y'=8] {'x'}, dimensions={0} | all-to-all | bytes 2359296 | tf_op jit(solution)/shard_map/all_to_all | solution.py:165
  61.1 0.0 all-gather.2.cloned.1.call-done.w_hbm
  61.1 1.9 %collective-permute-start = (bf16[32,9,16,128]{3,2,1,0:T(8,128)(2,1)S(1)}, bf16[32,9,16,128]{3,2,1,0:T(8,128)(2,1)}, u32[]{:S(2)}, u32[]{:S(2)}) collective-permute-start(bf16[32,9,16,128]{3,2,1,0:T(8,128)(2,1)S(1)} %bitcast.13), channel_id=1, source_target_pairs={{0,8},{8,0},{1,9},{9,1},{2,10},{10,2},{3,11},{11,3},{4,12},{12,4},... | collective-permute-start | bytes 3538952 | tf_op jit(solution)/shard_map/ppermute | solution.py:168
  63.1 0.0 copy-start.1
  63.1 1.2 copy-done.1
  64.3 2.3 %shard_map.71 = (f32[32,8,16,128]{3,2,1,0:T(8,128)S(1)}, f32[8,512,128]{2,1,0:T(8,128)S(1)}) custom-call(s32[1]{0:T(128)} %bitcast.me_ref, bf16[8,512,128]{2,1,0:T(8,128)(2,1)S(1)} %copy-done.1, bf16[32,9,16,128]{3,2,1,0:T(8,128)(2,1)S(1)} %bitcast.14), custom_call_target="tpu_custom_call" | custom-call | flops 1610612736 | bytes 6291456 | tf_op jit(solution)/shard_map/pallas_call | solution.py:122
  66.6 0.0 collective-permute-done.x_ref
  66.6 4.2 %shard_map.72 = (bf16[32,8,16,128]{3,2,1,0:T(8,128)(2,1)S(1)}, f32[8,512,128]{2,1,0:T(8,128)}) custom-call(s32[1]{0:T(128)} %bitcast.me_ref, bf16[8,512,128]{2,1,0:T(8,128)(2,1)S(1)} %copy-done.1, bf16[32,9,16,128]{3,2,1,0:T(8,128)(2,1)} %collective-permute-done.x_ref, f32[8,512,128]{2,1,0:T(8,128)S(1)} %get-tuple-element.11.refs_0_), custom_call_target="tpu_custom_call" | custom-call | flops 1610612736 | bytes 6291456 | tf_op jit(solution)/shard_map/pallas_call | solution.py:122
  70.8 0.0 reduce-scatter.2.cloned.1.call-update
  70.8 2.4 %collective-permute-start.1 = (bf16[32,8,16,128]{3,2,1,0:T(8,128)(2,1)S(1)}, bf16[32,8,16,128]{3,2,1,0:T(8,128)(2,1)S(1)}, u32[]{:S(2)}, u32[]{:S(2)}) collective-permute-start(bf16[32,8,16,128]{3,2,1,0:T(8,128)(2,1)S(1)} %get-tuple-element.12), channel_id=1, source_target_pairs={{0,8},{8,0},{1,9},{9,1},{2,10},{10,2},{3,11},{11,3},{4,12},{12,4},... | collective-permute-start | bytes 3145736 | tf_op jit(solution)/shard_map/ppermute | solution.py:172
  73.2 2.3 %collective-permute-done.1 = bf16[32,8,16,128]{3,2,1,0:T(8,128)(2,1)S(1)} collective-permute-done((bf16[32,8,16,128]{3,2,1,0:T(8,128)(2,1)S(1)}, bf16[32,8,16,128]{3,2,1,0:T(8,128)(2,1)S(1)}, u32[]{:S(2)}, u32[]{:S(2)}) %collective-permute-start.1) | collective-permute-done | bytes 1048608 | tf_op jit(solution)/shard_map/ppermute | solution.py:172
  75.5 0.4 add_convert_fusion
  75.9 18.3 %all_to_all.27 = bf16[4,64,16,128]{3,2,1,0:T(8,128)(2,1)S(1)} all-to-all(bf16[4,64,16,128]{3,2,1,0:T(8,128)(2,1)S(1)} %bitcast.16), channel_id=1, replica_groups=mesh['x'=4,'z'=8,'c'=2,'y'=8] {'x'}, dimensions={0} | all-to-all | bytes 2097152 | tf_op jit(solution)/shard_map/all_to_all | solution.py:139
  94.2 0.3 reduce_sum.24
  94.5 22.5 %all_to_all.28 = bf16[64,16,128]{2,1,0:T(8,128)(2,1)S(1)} all-to-all(bf16[64,16,128]{2,1,0:T(8,128)(2,1)S(1)} %reduce_sum.24), channel_id=1, replica_groups=mesh['x'=4,'z'=8,'c'=2,'y'=8] {'z','y'}, dimensions={0} | all-to-all | bytes 524288 | tf_op jit(solution)/shard_map/all_to_all | solution.py:177
  116.9 0.7 bitcast_reduce_fusion
  117.6 0.0 reduce-scatter.2.cloned.1.call-done
  117.6 1.6 %multiply_convert_fusion = bf16[1,512,128]{2,1,0:T(8,128)(2,1)} fusion(f32[1,512,128]{2,1,0:T(8,128)} %reduce-scatter.2.cloned.1.call-done), kind=kLoop, calls=%fused_computation.2 | loop fusion | flops 131072 | bytes 393216 | tf_op jit(solution)/shard_map/convert_element_type | solution.py:179
  (1 shorter events, 0.0 us)
Async XLA Ops:
  7.2 54.0 %all-gather.2.cloned.1.call-start = ((), (), s32[]{:S(2)}) async-start(), calls=%async_computation.6 | async-start | bytes 1179648 | tf_op jit(solution)/shard_map/all_gather | solution.py:152
  7.9 15.1 %all-to-all-start = ((bf16[8,16,128]{2,1,0:T(8,128)(2,1)}), bf16[8,16,128]{2,1,0:T(8,128)(2,1)S(1)}, u32[]{:S(2)}, u32[]{:S(2)}) async-start(bf16[8,16,128]{2,1,0:T(8,128)(2,1)} %bitcast.20), calls=%async_computation | async-start | bytes 65536 | tf_op jit(solution)/shard_map/all_to_all | solution.py:155
  15.0 102.6 %reduce-scatter.2.cloned.1.call-start = ((), (), s32[]{:S(2)}) async-start(), calls=%async_computation.7 | async-start | bytes 2359296 | tf_op jit(solution)/shard_map/reduce_scatter | solution.py:174
  23.0 0.7 copy-start
  61.1 5.5 %collective-permute-start = (bf16[32,9,16,128]{3,2,1,0:T(8,128)(2,1)S(1)}, bf16[32,9,16,128]{3,2,1,0:T(8,128)(2,1)}, u32[]{:S(2)}, u32[]{:S(2)}) collective-permute-start(bf16[32,9,16,128]{3,2,1,0:T(8,128)(2,1)S(1)} %bitcast.13), channel_id=1, source_target_pairs={{0,8},{8,0},{1,9},{9,1},{2,10},{10,2},{3,11},{11,3},{4,12},{12,4},... | collective-permute-start | bytes 3538952 | tf_op jit(solution)/shard_map/ppermute | solution.py:168
  63.1 1.2 copy-start.1
  70.8 4.7 %collective-permute-start.1 = (bf16[32,8,16,128]{3,2,1,0:T(8,128)(2,1)S(1)}, bf16[32,8,16,128]{3,2,1,0:T(8,128)(2,1)S(1)}, u32[]{:S(2)}, u32[]{:S(2)}) collective-permute-start(bf16[32,8,16,128]{3,2,1,0:T(8,128)(2,1)S(1)} %get-tuple-element.12), channel_id=1, source_target_pairs={{0,8},{8,0},{1,9},{9,1},{2,10},{10,2},{3,11},{11,3},{4,12},{12,4},... | collective-permute-start | bytes 3145736 | tf_op jit(solution)/shard_map/ppermute | solution.py:172
Sparse Core Ops, SparseCore 0:
  10.1 45.4 all-gather.1
  71.0 41.9 reduce-scatter.1

commit v4 on v3

--- a/solution.py
+++ b/solution.py
@@ -55,14 +55,22 @@
     )(*blocks)
 
 
-def main_kernel(n_pos, first, me_ref, w_hbm, x_ref, *refs):
+def main_kernel(n_pos, first, me_ref, w_hbm, x_in, *refs):
     if first:
         ig_ref, wg_ref, w_ref, w_sem = refs
+        x_ref = x_in
     else:
-        wg_in_ref, ig_ref, wg_hbm, w_ref, w_sem, wg_ref, wg_sem = refs
+        wg_in_ref, ig_ref, wg_hbm, w_ref, w_sem, wg_ref, wg_sem, x_ref, x_sem = refs
     get = pltpu.make_async_copy(w_hbm, w_ref, w_sem)
+    tiles, feats = x_ref.shape[0], x_ref.shape[1] - 1
+    if not first:
+        get_facts = pltpu.make_async_copy(x_in.at[:, pl.ds(feats, 1)], x_ref.at[:, pl.ds(feats, 1)], x_sem.at[0])
+        get_rows = pltpu.make_async_copy(x_in.at[:, pl.ds(0, feats)], x_ref.at[:, pl.ds(0, feats)], x_sem.at[1])
+        get_facts.start()
+        get_rows.start()
     get.start()
-    tiles, feats = x_ref.shape[0], x_ref.shape[1] - 1
+    if not first:
+        get_facts.wait()
     rows = tiles * x_ref.shape[2]
     labels = w_ref.shape[1]
 
@@ -78,6 +86,8 @@
     words = jnp.zeros((labels // 32, rows), jnp.int32)
     for p in range(n_pos):
         words = words | jnp.where(word[p : p + 1] == lines, bit[p : p + 1], 0)
+    if not first:
+        get_rows.wait()
     x = jnp.concatenate([x_ref[:, f].reshape(rows, 128) for f in range(feats)], axis=1)
 
     get.wait()
@@ -119,13 +129,14 @@
     scratch = [pltpu.VMEM((feats, labels, 128), jnp.bfloat16), pltpu.SemaphoreType.DMA]
     if not first:
         scratch += [pltpu.VMEM((feats, labels, 128), jnp.float32), pltpu.SemaphoreType.DMA((feats // 2,))]
+        scratch += [pltpu.VMEM(x.shape, jnp.bfloat16), pltpu.SemaphoreType.DMA((2,))]
     return pl.pallas_call(
         functools.partial(main_kernel, n_pos, first),
         out_shape=(
             jax.ShapeDtypeStruct((blocks, feats, sub, 128), out_type),
             jax.ShapeDtypeStruct((feats, labels, 128), jnp.float32),
         ),
-        in_specs=[smem, hbm, vmem] + [vmem] * (not first),
+        in_specs=[smem, hbm, vmem] if first else [smem, hbm, hbm, vmem],
         out_specs=(vmem, vmem if first else hbm),
         scratch_shapes=scratch,
         compiler_params=pltpu.CompilerParams(vmem_limit_bytes=28 * 1024 * 1024),

time: 127 us -> 126 us (level)
  no operation moved by 1% of the time
where the time goes in v4:
time: 126 us
  blocking collectives  77.9 us (62%)
  between operations  14.1 us (11%)
  starting transfers between devices  11.5 us (9%)
  waiting for transfers between devices  9.3 us (7%)
  Pallas kernels  8.1 us (6%)
  other arithmetic  2.92 us (2%)
  local copies, waits for them, and re-layouts  1.9 us (2%)
    all_to_all x1, blocking collectives, shards(): lax.all_to_all(ig.astype(jnp.bfloat16), ('z', 'y'), split_axis=0, concat_...  22.4 us
    all_to_all x1, blocking collectives, shards(): lax.all_to_all(copies(NZ, own, facts[None]), 'z', split_axis=0, concat_ax...  21.3 us
    all_to_all x1, blocking collectives, collect(): lax.all_to_all(parts.astype(jnp.bfloat16), axis, split_axis=0, concat_axi...  18.3 us
    all_to_all x1, blocking collectives, shards(): lax.all_to_all(lines, 'x', split_axis=0, concat_axis=0, tiled=True)  16 us
    all_to_all x1, starting transfers between devices, shards(): lax.all_to_all(instances.reshape(ny, share, part), 'y', split_axis=0, con...  7.11 us
    all_to_all x1, waiting for transfers between devices, shards(): lax.all_to_all(instances.reshape(ny, share, part), 'y', split_axis=0, con...  6.34 us
    pallas_call x2, Pallas kernels, gradients(): pl.pallas_call(functools.partial(main_kernel, n_pos, first), out_shape=(j...  6.27 us
  transfers between devices with their start and end apart: 5, of which 2 were waited for; matrix products, arithmetic and copies ran while one was open for 1% of the time, Pallas kernels for 3%

profile of v4, /device:TPU:6, one launch (start us, length us, event | category | flops | bytes accessed | tf_op | source)
XLA Modules:
  0.0 125.8 jit_solution(14259703872197653387)
XLA Ops:
  7.2 0.0 all-gather.2.cloned.1.call-start
  7.2 0.7 all-gather.2.cloned.1.call-update
  7.9 7.1 %all-to-all-start = ((bf16[8,16,128]{2,1,0:T(8,128)(2,1)}), bf16[8,16,128]{2,1,0:T(8,128)(2,1)S(1)}, u32[]{:S(2)}, u32[]{:S(2)}) async-start(bf16[8,16,128]{2,1,0:T(8,128)(2,1)} %bitcast.20), calls=%async_computation | async-start | bytes 65536 | tf_op jit(solution)/shard_map/all_to_all | solution.py:166
  15.0 0.0 reduce-scatter.2.cloned.1.call-start
  15.1 1.6 %shard_map.68 = bf16[16,128]{1,0:T(8,128)(2,1)} custom-call(s32[1]{0:T(128)} %bitcast.2.place_ref, s32[128]{0:T(128)} %home_ref.1, s32[20,128]{1,0:T(8,128)} %bitcast.22, s32[32,128]{1,0:T(8,128)} %bitcast.21), custom_call_target="tpu_custom_call" | custom-call | tf_op jit(solution)/shard_map/pallas_call | solution.py:167
  16.7 6.3 %all-to-all-done.refs_0_ = bf16[8,16,128]{2,1,0:T(8,128)(2,1)S(1)} async-done(((bf16[8,16,128]{2,1,0:T(8,128)(2,1)}), bf16[8,16,128]{2,1,0:T(8,128)(2,1)S(1)}, u32[]{:S(2)}, u32[]{:S(2)}) %all-to-all-start) | async-done | bytes 32800 | tf_op jit(solution)/shard_map/all_to_all | solution.py:166
  23.0 0.0 copy-start
  23.0 0.7 copy-done
  23.8 21.3 %all_to_all.25.refs_0_ = bf16[8,9,16,128]{3,2,1,0:T(8,128)(2,1)S(1)} all-to-all(bf16[8,9,16,128]{3,2,1,0:T(8,128)(2,1)S(1)} %shard_map.69), channel_id=1, replica_groups=mesh['x'=4,'z'=8,'c'=2,'y'=8] {'z'}, dimensions={0} | all-to-all | bytes 589824 | tf_op jit(solution)/shard_map/all_to_all | solution.py:174
  45.0 0.2 shard_map.70
  45.2 16.0 %all_to_all.26 = bf16[4,8,9,16,128]{4,3,2,1,0:T(8,128)(2,1)S(1)} all-to-all(bf16[4,8,9,16,128]{4,3,2,1,0:T(8,128)(2,1)S(1)} %shard_map.70), channel_id=1, replica_groups=mesh['x'=4,'z'=8,'c'=2,'y'=8] {'x'}, dimensions={0} | all-to-all | bytes 2359296 | tf_op jit(solution)/shard_map/all_to_all | solution.py:176
  61.1 0.0 all-gather.2.cloned.1.call-done.w_hbm
  61.1 1.9 %collective-permute-start = (bf16[32,9,16,128]{3,2,1,0:T(8,128)(2,1)S(1)}, bf16[32,9,16,128]{3,2,1,0:T(8,128)(2,1)}, u32[]{:S(2)}, u32[]{:S(2)}) collective-permute-start(bf16[32,9,16,128]{3,2,1,0:T(8,128)(2,1)S(1)} %bitcast.13), channel_id=1, source_target_pairs={{0,8},{8,0},{1,9},{9,1},{2,10},{10,2},{3,11},{11,3},{4,12},{12,4},... | collective-permute-start | bytes 3538952 | tf_op jit(solution)/shard_map/ppermute | solution.py:179
  63.1 0.0 copy-start.1
  63.1 1.2 copy-done.1
  64.3 2.3 %shard_map.71 = (f32[32,8,16,128]{3,2,1,0:T(8,128)S(1)}, f32[8,512,128]{2,1,0:T(8,128)S(1)}) custom-call(s32[1]{0:T(128)} %bitcast.me_ref, bf16[8,512,128]{2,1,0:T(8,128)(2,1)S(1)} %copy-done.1, bf16[32,9,16,128]{3,2,1,0:T(8,128)(2,1)S(1)} %bitcast.14), custom_call_target="tpu_custom_call" | custom-call | flops 1610612736 | bytes 6291456 | tf_op jit(solution)/shard_map/pallas_call | solution.py:133
  66.6 0.0 collective-permute-done.x_in
  66.6 4.0 %shard_map.72 = (bf16[32,8,16,128]{3,2,1,0:T(8,128)(2,1)S(1)}, f32[8,512,128]{2,1,0:T(8,128)}) custom-call(s32[1]{0:T(128)} %bitcast.me_ref, bf16[8,512,128]{2,1,0:T(8,128)(2,1)S(1)} %copy-done.1, bf16[32,9,16,128]{3,2,1,0:T(8,128)(2,1)} %collective-permute-done.x_in, f32[8,512,128]{2,1,0:T(8,128)S(1)} %get-tuple-element.11.refs_0_), custom_call_target="tpu_custom_call" | custom-call | flops 1610612736 | bytes 6291456 | tf_op jit(solution)/shard_map/pallas_call | solution.py:133
  70.6 0.0 reduce-scatter.2.cloned.1.call-update
  70.6 2.4 %collective-permute-start.1 = (bf16[32,8,16,128]{3,2,1,0:T(8,128)(2,1)S(1)}, bf16[32,8,16,128]{3,2,1,0:T(8,128)(2,1)S(1)}, u32[]{:S(2)}, u32[]{:S(2)}) collective-permute-start(bf16[32,8,16,128]{3,2,1,0:T(8,128)(2,1)S(1)} %get-tuple-element.12), channel_id=1, source_target_pairs={{0,8},{8,0},{1,9},{9,1},{2,10},{10,2},{3,11},{11,3},{4,12},{12,4},... | collective-permute-start | bytes 3145736 | tf_op jit(solution)/shard_map/ppermute | solution.py:183
  73.0 2.3 %collective-permute-done.1 = bf16[32,8,16,128]{3,2,1,0:T(8,128)(2,1)S(1)} collective-permute-done((bf16[32,8,16,128]{3,2,1,0:T(8,128)(2,1)S(1)}, bf16[32,8,16,128]{3,2,1,0:T(8,128)(2,1)S(1)}, u32[]{:S(2)}, u32[]{:S(2)}) %collective-permute-start.1) | collective-permute-done | bytes 1048608 | tf_op jit(solution)/shard_map/ppermute | solution.py:183
  75.3 0.4 add_convert_fusion
  75.7 18.3 %all_to_all.27 = bf16[4,64,16,128]{3,2,1,0:T(8,128)(2,1)S(1)} all-to-all(bf16[4,64,16,128]{3,2,1,0:T(8,128)(2,1)S(1)} %bitcast.16), channel_id=1, replica_groups=mesh['x'=4,'z'=8,'c'=2,'y'=8] {'x'}, dimensions={0} | all-to-all | bytes 2097152 | tf_op jit(solution)/shard_map/all_to_all | solution.py:150
  94.0 0.3 reduce_sum.24
  94.3 22.4 %all_to_all.28 = bf16[64,16,128]{2,1,0:T(8,128)(2,1)S(1)} all-to-all(bf16[64,16,128]{2,1,0:T(8,128)(2,1)S(1)} %reduce_sum.24), channel_id=1, replica_groups=mesh['x'=4,'z'=8,'c'=2,'y'=8] {'z','y'}, dimensions={0} | all-to-all | bytes 524288 | tf_op jit(solution)/shard_map/all_to_all | solution.py:188
  116.6 0.7 bitcast_reduce_fusion
  117.3 0.0 reduce-scatter.2.cloned.1.call-done
  117.3 1.6 %multiply_convert_fusion = bf16[1,512,128]{2,1,0:T(8,128)(2,1)} fusion(f32[1,512,128]{2,1,0:T(8,128)} %reduce-scatter.2.cloned.1.call-done), kind=kLoop, calls=%fused_computation.2 | loop fusion | flops 131072 | bytes 393216 | tf_op jit(solution)/shard_map/convert_element_type | solution.py:190
  (1 shorter events, 0.0 us)
Async XLA Ops:
  7.2 54.0 %all-gather.2.cloned.1.call-start = ((), (), s32[]{:S(2)}) async-start(), calls=%async_computation.6 | async-start | bytes 1179648 | tf_op jit(solution)/shard_map/all_gather | solution.py:163
  7.9 15.1 %all-to-all-start = ((bf16[8,16,128]{2,1,0:T(8,128)(2,1)}), bf16[8,16,128]{2,1,0:T(8,128)(2,1)S(1)}, u32[]{:S(2)}, u32[]{:S(2)}) async-start(bf16[8,16,128]{2,1,0:T(8,128)(2,1)} %bitcast.20), calls=%async_computation | async-start | bytes 65536 | tf_op jit(solution)/shard_map/all_to_all | solution.py:166
  15.0 102.3 %reduce-scatter.2.cloned.1.call-start = ((), (), s32[]{:S(2)}) async-start(), calls=%async_computation.7 | async-start | bytes 2359296 | tf_op jit(solution)/shard_map/reduce_scatter | solution.py:185
  23.0 0.7 copy-start
  61.1 5.5 %collective-permute-start = (bf16[32,9,16,128]{3,2,1,0:T(8,128)(2,1)S(1)}, bf16[32,9,16,128]{3,2,1,0:T(8,128)(2,1)}, u32[]{:S(2)}, u32[]{:S(2)}) collective-permute-start(bf16[32,9,16,128]{3,2,1,0:T(8,128)(2,1)S(1)} %bitcast.13), channel_id=1, source_target_pairs={{0,8},{8,0},{1,9},{9,1},{2,10},{10,2},{3,11},{11,3},{4,12},{12,4},... | collective-permute-start | bytes 3538952 | tf_op jit(solution)/shard_map/ppermute | solution.py:179
  63.1 1.2 copy-start.1
  70.6 4.7 %collective-permute-start.1 = (bf16[32,8,16,128]{3,2,1,0:T(8,128)(2,1)S(1)}, bf16[32,8,16,128]{3,2,1,0:T(8,128)(2,1)S(1)}, u32[]{:S(2)}, u32[]{:S(2)}) collective-permute-start(bf16[32,8,16,128]{3,2,1,0:T(8,128)(2,1)S(1)} %get-tuple-element.12), channel_id=1, source_target_pairs={{0,8},{8,0},{1,9},{9,1},{2,10},{10,2},{3,11},{11,3},{4,12},{12,4},... | collective-permute-start | bytes 3145736 | tf_op jit(solution)/shard_map/ppermute | solution.py:183
Sparse Core Ops, SparseCore 0:
  10.1 45.4 all-gather.1
  70.7 41.8 reduce-scatter.1
